TPU v7x, 512 devices: a whole 4x8x8 slice. The times are simulated.
512 devices in a mesh: row: 32 (over x, y), col: 16 (over z, core).
Axes of the slice: x: 4, y: 8, z: 8, core: 2. Of those that a mesh axis runs over, the one named last changes fastest.
Arguments:
- points: float32 [64, 16384], P(None, ('row', 'col')), may hold values from -6 to 6
- length_scales: float32 [64], replicated, may hold values from 2 to 8
- variances: float32 [2], replicated, may hold values from 0.5 to 2
- targets: float32 [16384], P(('row', 'col')), may hold values from -6 to 6
- probe_vectors: float32 [30, 16384], P(None, ('row', 'col')), may hold values from -6 to 6
Outputs:
- solves: float32 [31, 16384], P(None, ('row', 'col'))
- gradient: float32 [66], replicated
All inputs are finite; a program needn't handle non-finite values.
Results may differ from a plain program's by a relative error of at most 0.0003.
Values sent between devices are 32-bit elements; how exact they have to be, the bound alone decides.
No kernel may reach another device: no remote copies, remote signals or barrier semaphores. Data moves between devices by JAX's collectives and lax.ppermute only.
A program may use at most 64 MiB of HBM per device.

v0:
```python
import jax
import jax.numpy as jnp
from jax import lax
from jax.sharding import PartitionSpec as P

PROBES = 30
ITERS = 2


highest = lax.Precision.HIGHEST
root_five = 5.0**0.5


def kernel_terms(left_points, right_points):
    squared = (
        jnp.sum(left_points * left_points, 0)[:, None]
        + jnp.sum(right_points * right_points, 0)[None, :]
        - 2.0 * jnp.einsum("fm,fn->mn", left_points, right_points, precision=highest)
    )
    scaled_dist = root_five * jnp.sqrt(jnp.maximum(squared, 0.0))
    decayed = jnp.exp(-scaled_dist)
    kernel_base = (1.0 + scaled_dist + scaled_dist * scaled_dist / 3.0) * decayed
    kernel_slope = 5.0 / 3.0 * (1.0 + scaled_dist) * decayed
    return (kernel_base, kernel_slope)


def split_blocks(array_in):
    column_count = array_in.shape[1]
    block_width = 128
    block_count = column_count // block_width
    return array_in.reshape(array_in.shape[0], block_count, block_width).transpose(1, 0, 2)


def gradient_terms(row_pts, block_points, weight_matrix):
    kernel_base, kernel_slope = kernel_terms(row_pts, block_points)
    weighted = weight_matrix * kernel_slope
    row_sums = jnp.sum(weighted, 1)
    col_sums = jnp.sum(weighted, 0)
    cross_term = jnp.einsum("mn,fn->fm", weighted, block_points, precision=highest)
    scale_terms = (
        jnp.sum(row_pts * row_pts * row_sums[None, :], 1)
        + jnp.sum(block_points * block_points * col_sums[None, :], 1)
        - 2.0 * jnp.sum(row_pts * cross_term, 1)
    )
    signal_term = jnp.sum(weight_matrix * kernel_base)
    return jnp.concatenate([scale_terms, signal_term[None]])


def sum_columns(row_points, col_piece, value_piece):

    def sum_block_step(running, members):
        kernel_base, unused = kernel_terms(row_points, members[0])
        return (running + jnp.einsum("mn,cn->cm", kernel_base, members[1], precision=highest), None)

    start_value = jnp.zeros((value_piece.shape[0], row_points.shape[1]), jnp.float32)
    running, unused = lax.scan(
        sum_block_step, start_value, (split_blocks(col_piece), split_blocks(value_piece))
    )
    return running


def gram_of(first_block, second_block):
    return jnp.einsum("cn,dn->cd", first_block, second_block, precision=highest)


def symmetric(matrix):
    return 0.5 * (matrix + matrix.T)


def solve_spd(matrix, right):
    lower = jnp.linalg.cholesky(matrix)
    return jax.scipy.linalg.cho_solve((lower, True), right)


def local(points, length_scales, variances, targets, probe_vectors):
    row_count = lax.axis_size("row")
    col_count = lax.axis_size("col")
    shard_width = points.shape[1]
    total_points = shard_width * row_count * col_count
    signal_var = variances[0]
    noise_var = variances[1]
    scaled = points / length_scales[:, None]
    rhs_block = jnp.concatenate([probe_vectors, targets[None, :]], 0)
    row_points = lax.all_gather(scaled, "col", axis=1, tiled=True)
    col_points = lax.all_gather(scaled, "row", axis=1, tiled=True)
    solves = jnp.zeros_like(rhs_block)
    residual = rhs_block
    direction = rhs_block
    res_gram = symmetric(lax.psum(gram_of(residual, residual), ("row", "col")))
    for iteration in range(ITERS):
        partial_value = sum_columns(
            row_points, col_points, lax.all_gather(direction, "row", axis=1, tiled=True)
        )
        summed = lax.psum_scatter(partial_value, "col", scatter_dimension=1, tiled=True)
        images = signal_var * summed + noise_var * direction
        curvature = symmetric(lax.psum(gram_of(direction, images), ("row", "col")))
        advance = solve_spd(curvature, res_gram)
        solves = solves + jnp.einsum("cd,cn->dn", advance, direction, precision=highest)
        residual = residual - jnp.einsum("cd,cn->dn", advance, images, precision=highest)
        if iteration + 1 < ITERS:
            next_gram = symmetric(lax.psum(gram_of(residual, residual), ("row", "col")))
            carry_over = solve_spd(res_gram, next_gram)
            direction = residual + jnp.einsum("cd,cn->dn", carry_over, direction, precision=highest)
            res_gram = next_gram
    column_weights = jnp.concatenate(
        [jnp.full((PROBES,), -1.0 / PROBES, jnp.float32), jnp.ones((1,), jnp.float32)]
    )
    row_weights = solves * column_weights[:, None] * (0.5 / total_points)
    pair_block = jnp.concatenate([rhs_block[:PROBES], solves[PROBES:]], 0)
    row_left = lax.all_gather(row_weights, "col", axis=1, tiled=True)
    start_value = jnp.zeros((points.shape[0] + 1,), jnp.float32)

    def add_block_step(totals, members):
        block_points, block_vals = members
        weight_matrix = jnp.einsum("cm,cn->mn", row_left, block_vals, precision=highest)
        return (totals + gradient_terms(row_points, block_points, weight_matrix), None)

    totals, unused = lax.scan(
        add_block_step,
        start_value,
        (
            split_blocks(col_points),
            split_blocks(lax.all_gather(pair_block, "row", axis=1, tiled=True)),
        ),
    )
    noise_term = noise_var * jnp.sum(row_weights * pair_block)
    gradient = lax.psum(jnp.concatenate([signal_var * totals, noise_term[None]]), ("row", "col"))
    return (solves, gradient)


def solution(mesh):
    placed = (P(None, ("row", "col")), P(), P(), P(("row", "col")), P(None, ("row", "col")))
    return jax.shard_map(
        local, mesh=mesh, in_specs=placed, out_specs=(P(None, ("row", "col")), P()), check_vma=False
    )
```

profile of v0, /device:TPU:1, one launch (start us, length us, event | category | flops | bytes accessed | tf_op | source)
XLA Modules:
  0.0 816.9 jit_solution(2267678056265936391)
XLA Ops:
  7.8 0.7 broadcast_divide_fusion
  8.5 25.2 %all_gather.19 = f32[64,512]{0,1:T(8,128)S(1)} all-gather(f32[64,32]{0,1:T(8,128)S(1)} %broadcast_divide_fusion), channel_id=1, replica_groups=mesh['row'=32,'col'=16] {'col'}, dimensions={1}, use_global_device_ids=true | all-gather | bytes 139264 | tf_op jit(solution)/shard_map/all_gather | solution.py:84
  34.0 38.8 %all_gather.20 = f32[64,1024]{0,1:T(8,128)S(1)} all-gather(f32[64,32]{0,1:T(8,128)S(1)} %broadcast_divide_fusion), channel_id=1, replica_groups=mesh['row'=32,'col'=16] {'row'}, dimensions={1}, use_global_device_ids=true | all-gather | bytes 270336 | tf_op jit(solution)/shard_map/all_gather | solution.py:85
  72.8 0.7 copy-done.4
  73.7 36.1 %all_gather.18 = f32[31,1024]{0,1:T(8,128)S(1)} all-gather(f32[31,32]{0,1:T(8,128)S(1)} %copy.19), channel_id=1, replica_groups=mesh['row'=32,'col'=16] {'row'}, dimensions={1}, use_global_device_ids=true | all-gather | bytes 130944 | tf_op jit(solution)/shard_map/all_gather | solution.py:92
  110.0 7.1 while.38
  117.2 0.8 copy.39
  119.5 72.8 %reduce-scatter.7.cloned.1.call-done = f32[32,31]{1,0:T(8,128)} async-done(((f32[512,31]{1,0:T(8,128)}), f32[32,31]{1,0:T(8,128)}) %reduce-scatter.7.cloned.1.call-update) | async-done | bytes 3984
  192.3 0.8 copy.40
  193.1 1.3 fusion.91
  194.5 99.9 %all-reduce = (f32[31,31]{1,0:T(8,128)S(1)}, f32[31,31]{1,0:T(8,128)S(1)}) all-reduce(f32[31,31]{1,0:T(8,128)S(1)} %fusion.105, f32[31,31]{1,0:T(8,128)S(1)} %fusion.91), channel_id=1, replica_groups=mesh['row'=32,'col'=16] {'row','col'}, use_global_device_ids=true, to_apply=%region_8.10 | all-reduce | flops 1922 | bytes 15376 | tf_op jit(solution)/shard_map/psum | solution.py:89
  294.6 2.8 cholesky.59
  298.1 0.7 fusion.65
  298.8 2.4 custom-call.12
  301.6 1.4 convolution_subtract_fusion
  303.2 94.4 %psum.37 = f32[31,31]{1,0:T(8,128)S(1)} all-reduce(f32[31,31]{1,0:T(8,128)S(1)} %fusion.107), channel_id=1, replica_groups=mesh['row'=32,'col'=16] {'row','col'}, use_global_device_ids=true, to_apply=%region_9.12 | all-reduce | flops 961 | bytes 7688 | tf_op jit(solution)/shard_map/psum | solution.py:101
  397.7 2.8 cholesky.70
  401.2 0.7 fusion.66
  401.9 2.4 custom-call.13
  404.9 36.3 %all_gather.21 = f32[31,1024]{0,1:T(8,128)S(1)} all-gather(f32[31,32]{0,1:T(8,128)S(1)} %copy.28), channel_id=1, replica_groups=mesh['row'=32,'col'=16] {'row'}, dimensions={1}, use_global_device_ids=true | all-gather | bytes 130944 | tf_op jit(solution)/shard_map/all_gather | solution.py:92
  441.5 7.1 while.39
  448.6 0.8 copy.41
  449.7 65.7 %reduce-scatter.9.cloned.1.call-done = f32[32,31]{1,0:T(8,128)} async-done(((f32[512,31]{1,0:T(8,128)}), f32[32,31]{1,0:T(8,128)}) %reduce-scatter.9.cloned.1.call-update) | async-done | bytes 3984
  515.3 0.8 copy.42
  516.1 1.3 fusion.87
  517.5 99.8 %psum.38 = f32[31,31]{1,0:T(8,128)S(1)} all-reduce(f32[31,31]{1,0:T(8,128)S(1)} %fusion.87), channel_id=1, replica_groups=mesh['row'=32,'col'=16] {'row','col'}, use_global_device_ids=true, to_apply=%region_14.17 | all-reduce | flops 961 | bytes 7688 | tf_op jit(solution)/shard_map/psum | solution.py:96
  617.5 2.8 cholesky.81
  621.0 0.7 fusion.67
  621.6 2.4 custom-call.14
  625.3 0.7 multiply_reduce_fusion.3
  627.2 16.7 %all_gather.23 = f32[31,512]{0,1:T(8,128)S(1)} all-gather(f32[31,32]{0,1:T(8,128)S(1)} %copy.35), channel_id=1, replica_groups=mesh['row'=32,'col'=16] {'col'}, dimensions={1}, use_global_device_ids=true | all-gather | bytes 67456 | tf_op jit(solution)/shard_map/all_gather | solution.py:110
  644.0 36.5 %all_gather.22 = f32[31,1024]{0,1:T(8,128)S(1)} all-gather(f32[31,32]{0,1:T(8,128)S(1)} %copy.33), channel_id=1, replica_groups=mesh['row'=32,'col'=16] {'row'}, dimensions={1}, use_global_device_ids=true | all-gather | bytes 130944 | tf_op jit(solution)/shard_map/all_gather | solution.py:123
  680.7 23.8 %while.40 = (s32[]{:T(128)}, f32[65]{0:T(128)S(1)}, f32[8,31,128]{2,1,0:T(8,128)S(1)}, f32[31,512]{1,0:T(8,128)S(1)}, f32[512]{0:T(512)S(1)}, /*index=5*/f32[8,6...) while((s32[]{:T(128)}, f32[65]{0:T(128)S(1)}, ...), condition=%wide.region_23.26_spmd.clone, body=%wide.region_15.25_spmd.clone.sunk | while | flops 126721472 | bytes 1927835 | solution.py:118
  681.2 1.1 fusion.168
  683.0 0.6 fusion.170
  684.2 1.1 fusion.168
  686.0 0.6 fusion.170
  687.2 1.1 fusion.168
  688.9 0.6 fusion.170
  690.1 1.1 fusion.168
  693.1 1.1 fusion.168
  694.9 0.6 fusion.170
  696.1 1.1 fusion.168
  697.8 0.6 fusion.170
  699.0 1.1 fusion.168
  702.0 1.1 fusion.168
  704.4 0.6 broadcast_multiply_fusion
  705.2 104.9 %psum.39 = f32[66]{0:T(128)} all-reduce(f32[66]{0:T(128)S(1)} %pad_maximum_fusion.2), channel_id=1, replica_groups=mesh['row'=32,'col'=16] {'row','col'}, use_global_device_ids=true, to_apply=%region_25.28 | all-reduce | flops 66 | bytes 528 | tf_op jit(solution)/shard_map/psum | solution.py:127
  (162 shorter events, 34.1 us)
Async XLA Ops:
  7.2 0.7 copy-start.3
  7.2 185.1 %reduce-scatter.7.cloned.1.call-start = ((), (), s32[]{:S(2)}) async-start(), calls=%async_computation.2 | async-start | bytes 278528
  34.0 38.8 %copy-start = (f32[30,32]{1,0:T(8,128)S(1)}, f32[30,32]{1,0:T(8,128)}, u32[]{:S(2)}) copy-start(f32[30,32]{1,0:T(8,128)} %param.18) | copy-start | bytes 11524
  72.8 0.7 copy-start.4
  118.0 397.3 %reduce-scatter.9.cloned.1.call-start = ((), (), s32[]{:S(2)}) async-start(), calls=%async_computation.3 | async-start | bytes 278528
  118.3 0.7 copy-start.2
  624.6 1.3 copy-start.1
  624.6 0.7 copy-start.5
Sparse Core Ops, SparseCore 0:
  118.2 74.1 reduce-scatter.6
  449.6 65.7 reduce-scatter.8
where the time goes:
time: 818 us; the launch traced here: 817 us
  blocking collectives  588 us (72%)
  waiting for transfers between devices  139 us (17%)
  matrix products  35.7 us (4%)
  other arithmetic  29.6 us (4%)
  between operations  15.4 us (2%)
  local copies, waits for them, and re-layouts  8.34 us (1%)
    unnamed x4, waiting for transfers between devices  139 us
    psum x1, blocking collectives, local(): lax.psum(jnp.concatenate([signal_var * totals, noise_term[None]]), ('row'...  105 us
    psum x1, blocking collectives, local(): res_gram = symmetric(lax.psum(gram_of(residual, residual), ('row', 'col')))  99.9 us
    psum x1, blocking collectives, local(): curvature = symmetric(lax.psum(gram_of(direction, images), ('row', 'col')))  99.8 us
    psum x1, blocking collectives, local(): next_gram = symmetric(lax.psum(gram_of(residual, residual), ('row', 'col')))  94.4 us
    all_gather x2, blocking collectives, local(): lax.all_gather(direction, 'row', axis=1, tiled=True)  72.4 us
    all_gather x1, blocking collectives, local(): col_points = lax.all_gather(scaled, 'row', axis=1, tiled=True)  38.8 us
    all_gather x1, blocking collectives, local(): lax.all_gather(pair_block, 'row', axis=1, tiled=True)  36.5 us
  transfers between devices with their start and end apart: 2, of which 2 were waited for; matrix products, arithmetic and copies ran while one was open for 0% of the time, Pallas kernels for 0%

commit v1 on v0

v1 whole, which is shorter than its diff:
```python
import jax
import jax.numpy as jnp
from jax import lax
from jax.sharding import PartitionSpec as P

PROBES = 30
COLS = 31
FEAT = 64

highest = lax.Precision.HIGHEST
root_five = 5.0**0.5


def mul(spec, left, right):
    return jnp.einsum(spec, left, right, precision=highest, preferred_element_type=jnp.float32)


def kernel_terms(left_points, right_points):
    squared = (
        jnp.sum(left_points * left_points, 1)[:, None]
        + jnp.sum(right_points * right_points, 1)[None, :]
        - 2.0 * mul("mf,nf->mn", left_points, right_points)
    )
    scaled_dist = root_five * jnp.sqrt(jnp.maximum(squared, 0.0))
    decayed = jnp.exp(-scaled_dist)
    kernel_base = (1.0 + scaled_dist + scaled_dist * scaled_dist / 3.0) * decayed
    kernel_slope = 5.0 / 3.0 * (1.0 + scaled_dist) * decayed
    return (kernel_base, kernel_slope)


def symmetric(matrix):
    return 0.5 * (matrix + matrix.T)


def solve_spd(matrix, right):
    lower = jnp.linalg.cholesky(matrix)
    return jax.scipy.linalg.cho_solve((lower, True), right)


def gather_blocks(block, axis):
    count = lax.axis_size(axis)
    spread = jnp.broadcast_to(block[None], (count,) + block.shape)
    return lax.all_to_all(spread, axis, 0, 0, tiled=True)


def sum_blocks(block, axis):
    return jnp.sum(gather_blocks(block, axis), 0)


def lanes(*pieces):
    rows = pieces[0].shape[0]
    used = sum(p.shape[1] for p in pieces)
    return jnp.concatenate(list(pieces) + [jnp.zeros((rows, 128 - used), jnp.float32)], 1)


def square32(matrix):
    return jnp.pad(matrix, ((0, 1), (0, 1)))


def local(points, length_scales, variances, targets, probe_vectors):
    row_count = lax.axis_size("row")
    col_count = lax.axis_size("col")
    width = points.shape[1]
    total_points = width * row_count * col_count
    signal_var = variances[0]
    noise_var = variances[1]
    scaled = (points / length_scales[:, None]).T
    rhs = jnp.concatenate([probe_vectors, targets[None, :]], 0).T
    own = lanes(scaled, rhs)
    row_pack = gather_blocks(own, "col").reshape(col_count * width, 128)
    col_pack = gather_blocks(own, "row").reshape(row_count * width, 128)
    row_x, row_b = row_pack[:, :FEAT], row_pack[:, FEAT : FEAT + COLS]
    col_x, col_b = col_pack[:, :FEAT], col_pack[:, FEAT : FEAT + COLS]
    base, slope = kernel_terms(row_x, col_x)

    partial = mul("mn,nc->mc", base, col_b)
    part_curv = mul("mc,md->cd", row_b, partial)
    part_gram = mul("mc,md->cd", rhs, rhs)
    chunks = jnp.pad(partial, ((0, 0), (0, 1))).reshape(col_count, width, 32)
    grams = jnp.concatenate([square32(part_curv), square32(part_gram)], 1)
    message = jnp.concatenate(
        [chunks, jnp.broadcast_to(grams[None], (col_count, 32, 64)), jnp.zeros((col_count, 32, 32), jnp.float32)], 2
    )
    summed = jnp.sum(lax.all_to_all(message, "col", 0, 0, tiled=True), 0)
    images = signal_var * summed[:, :COLS] + noise_var * rhs
    shared = lanes(jnp.pad(images, ((0, 0), (0, 1))), summed[:, 32:96])
    col_got = gather_blocks(shared, "row")
    row_got = gather_blocks(jnp.pad(images, ((0, 0), (0, 1))), "col")
    col_v = col_got[:, :, :COLS].reshape(row_count * width, COLS)
    row_v = row_got[:, :, :COLS].reshape(col_count * width, COLS)
    grams = jnp.sum(col_got[:, :, 32:96], 0)
    res_gram = symmetric(grams[:COLS, 32 : 32 + COLS])
    curvature = symmetric(signal_var * grams[:COLS, :COLS] + noise_var * res_gram)
    advance = solve_spd(curvature, res_gram)

    def residual_of(rhs_part, image_part):
        return rhs_part - mul("nc,cd->nd", image_part, advance)

    row_r, col_r, own_r = residual_of(row_b, row_v), residual_of(col_b, col_v), residual_of(rhs, images)
    product = mul("mn,nc->mc", base, col_r)
    message = lanes(
        square32(mul("mc,md->cd", row_r, product)),
        square32(mul("mc,md->cd", own_r, own_r)),
        square32(mul("mc,md->cd", images, own_r)),
    )
    sums = sum_blocks(sum_blocks(message, "col"), "row")
    next_gram = symmetric(sums[:COLS, 32 : 32 + COLS])
    cross = sums[:COLS, 64 : 64 + COLS]
    carry_over = solve_spd(res_gram, next_gram)
    mixed = mul("cd,ce->de", cross, carry_over)
    next_curv = symmetric(
        signal_var * sums[:COLS, :COLS]
        + noise_var * next_gram
        + mixed
        + mixed.T
        + mul("cd,ce->de", carry_over, mul("cd,de->ce", curvature, carry_over))
    )
    next_advance = solve_spd(next_curv, next_gram)
    rhs_coef = advance + mul("cd,de->ce", carry_over, next_advance)

    def solves_of(rhs_part, res_part, cut=slice(None)):
        return mul("nc,cd->nd", rhs_part, rhs_coef[:, cut]) + mul("nc,cd->nd", res_part, next_advance[:, cut])

    own_s, row_s = solves_of(rhs, own_r), solves_of(row_b, row_r)
    col_s = solves_of(col_b, col_r, slice(PROBES, COLS))
    weights = jnp.where(jnp.arange(COLS) < PROBES, -1.0 / PROBES, 1.0) * (0.5 / total_points)
    row_w = row_s * weights[None, :]
    col_pair = jnp.concatenate([col_b[:, :PROBES], col_s], 1)
    matrix = mul("mc,nc->mn", row_w, col_pair)
    weighted = matrix * slope
    right = jnp.concatenate([col_x, col_x * col_x, jnp.ones((col_x.shape[0], 1), jnp.float32)], 1)
    moved = mul("mn,nf->mf", weighted, right)
    scale_terms = jnp.sum(
        row_x * row_x * moved[:, 2 * FEAT :] + moved[:, FEAT : 2 * FEAT] - 2.0 * row_x * moved[:, :FEAT], 0
    )
    signal_term = jnp.sum(matrix * base)
    noise_term = noise_var * jnp.sum(own_s * weights[None, :] * jnp.concatenate([rhs[:, :PROBES], own_s[:, PROBES:]], 1))
    terms = jnp.concatenate(
        [signal_var * scale_terms, (signal_var * signal_term)[None], noise_term[None], jnp.zeros((62,), jnp.float32)]
    )
    gradient = sum_blocks(sum_blocks(terms[None], "col"), "row")[0, : FEAT + 2]
    return (own_s.T, gradient)


def solution(mesh):
    placed = (P(None, ("row", "col")), P(), P(), P(("row", "col")), P(None, ("row", "col")))
    return jax.shard_map(
        local, mesh=mesh, in_specs=placed, out_specs=(P(None, ("row", "col")), P()), check_vma=False
    )
```

time: 818 us -> 220 us (0.27)
  blocking collectives: 588 us -> 51.5 us
  waiting for transfers between devices: 139 us -> 62.6 us
  starting transfers between devices: 0.08 us -> 34.1 us
  between operations: 15.4 us -> 4.27 us
  matrix products: 35.7 us -> 27.5 us
    psum x4 -> x0, blocking collectives: 399 us -> none  [the longest x1 105 us: local(): lax.psum(jnp.concatenate([signal_var * totals, noise_term[None]]), ('row'...]
    all_gather x6 -> x0, blocking collectives: 190 us -> none  [the longest x2 72.4 us: local(): lax.all_gather(direction, 'row', axis=1, tiled=True)]
    unnamed x4 -> x0, waiting for transfers between devices: 139 us -> none
    all_to_all x0 -> x6, waiting for transfers between devices: none -> 62.6 us  [the longest x5 51.3 us: gather_blocks(): return lax.all_to_all(spread, axis, 0, 0, tiled=True)]
    all_to_all x0 -> x3, blocking collectives: none -> 51.5 us  [gather_blocks(): return lax.all_to_all(spread, axis, 0, 0, tiled=True)]
    all_to_all x0 -> x6, starting transfers between devices: none -> 34.1 us  [the longest x5 29.8 us: gather_blocks(): return lax.all_to_all(spread, axis, 0, 0, tiled=True)]
    dot_general x64 -> x23, matrix products: 34.6 us -> 26.2 us  [mul(): jnp.einsum(spec, left, right, precision=highest, preferred_element_type=j...]
  transfers between devices with their start and end apart: 2 -> 6, of which waited for: 2 -> 6; matrix products, arithmetic and copies ran while one was open for 0% -> 5% of each run, Pallas kernels for 0% -> 0%
where the time goes in v1:
time: 220 us; the launch traced here: 219 us
  waiting for transfers between devices  62.6 us (28%)
  blocking collectives  51.5 us (23%)
  starting transfers between devices  34.1 us (16%)
  matrix products  27.5 us (12%)
  other arithmetic  26.6 us (12%)
  local copies, waits for them, and re-layouts  12.7 us (6%)
  between operations  4.27 us (2%)
    all_to_all x3, blocking collectives, gather_blocks(): return lax.all_to_all(spread, axis, 0, 0, tiled=True)  51.5 us
    all_to_all x5, waiting for transfers between devices, gather_blocks(): return lax.all_to_all(spread, axis, 0, 0, tiled=True)  51.3 us
    all_to_all x5, starting transfers between devices, gather_blocks(): return lax.all_to_all(spread, axis, 0, 0, tiled=True)  29.8 us
    dot_general x23, matrix products, mul(): jnp.einsum(spec, left, right, precision=highest, preferred_element_type=j...  26.2 us
    all_to_all x1, waiting for transfers between devices, local(): summed = jnp.sum(lax.all_to_all(message, 'col', 0, 0, tiled=True), 0)  11.3 us
    another operation x9, other arithmetic, solve_spd(): lower = jnp.linalg.cholesky(matrix)  10.6 us
    another operation x6, other arithmetic, solve_spd(): return jax.scipy.linalg.cho_solve((lower, True), right)  9 us
    unnamed x18, local copies, waits for them, and re-layouts  4.82 us
  transfers between devices with their start and end apart: 6, of which 6 were waited for; matrix products, arithmetic and copies ran while one was open for 5% of the time, Pallas kernels for 0%

profile of v1, /device:TPU:1, one launch (start us, length us, event | category | flops | bytes accessed | tf_op | source)
XLA Modules:
  0.0 219.3 jit_solution(6691427929949494927)
XLA Ops:
  0.6 0.7 copy.106
  1.4 0.8 copy.105
  2.2 0.7 divide_bitcast_fusion
  3.2 23.3 %all_to_all.45 = f32[16,32,128]{2,1,0:T(8,128)S(1)} all-to-all(f32[16,32,128]{2,1,0:T(8,128)S(1)} %broadcast_in_dim.43), channel_id=1, replica_groups=mesh['row'=32,'col'=16] {'col'}, dimensions={0} | all-to-all | bytes 524288 | tf_op jit(solution)/shard_map/all_to_all | solution.py:43
  26.5 0.8 broadcast_in_dim.44
  27.3 9.7 %all-to-all-start.1 = ((f32[32,32,128]{2,1,0:T(8,128)}), f32[32,32,128]{2,1,0:T(8,128)S(1)}, u32[]{:S(2)}, u32[]{:S(2)}) async-start(f32[32,32,128]{2,1,0:T(8,128)} %broadcast_in_dim.44), calls=%async_computation.1 | async-start | bytes 1048576 | tf_op jit(solution)/shard_map/all_to_all | solution.py:43
  37.5 16.0 %all-to-all-done.1 = f32[32,32,128]{2,1,0:T(8,128)S(1)} async-done(((f32[32,32,128]{2,1,0:T(8,128)}), f32[32,32,128]{2,1,0:T(8,128)S(1)}, u32[]{:S(2)}, u32[]{:S(2)}) %all-to-all-start.1) | async-done | bytes 524320 | tf_op jit(solution)/shard_map/all_to_all | solution.py:43
  53.7 2.5 %sqrt_multiply_fusion = f32[512,1024]{1,0:T(8,128)S(1)} fusion(f32[1024]{0:T(1024)S(1)} %get-tuple-element.18, f32[512]{0:T(512)S(1)} %multiply_reduce_fusion.1, f32[512,128]{1,0:T(8,128)S(1)} %bitcast.137, f32[1024,128]{1,0:T(8,128)S(1)} %bitcast.131), kind=kOutput, calls=%fused_computation.7 | convolution fusion | flops 405274624 | bytes 2889728 | tf_op jit(solution)/shard_map/mf,nf->mn/dot_general | solution.py:15
  56.3 1.3 copy-done
  57.6 2.5 %fusion.14 = f32[512,31]{0,1:T(8,128)S(1)} fusion(f32[512,1024]{1,0:T(8,128)S(1)} %sqrt_multiply_fusion, f32[1024,128]{1,0:T(8,128)S(1)} %bitcast.132), kind=kOutput, calls=%fused_computation.26 | convolution fusion | flops 198180864 | bytes 2684928 | tf_op jit(solution)/shard_map/mn,nc->mc/dot_general | solution.py:15
  60.2 0.7 fusion.70
  61.1 0.9 maximum_maximum_fusion
  62.0 4.4 %all-to-all-start.2 = ((f32[16,32,128]{2,1,0:T(8,128)}), f32[16,32,128]{2,1,0:T(8,128)S(1)}, u32[]{:S(2)}, u32[]{:S(2)}) async-start(f32[16,32,128]{2,1,0:T(8,128)} %maximum_maximum_fusion), calls=%async_computation.2 | async-start | bytes 524288 | tf_op jit(solution)/shard_map/all_to_all | solution.py:84
  66.9 11.3 %all-to-all-done.2 = f32[16,32,128]{2,1,0:T(8,128)S(1)} async-done(((f32[16,32,128]{2,1,0:T(8,128)}), f32[16,32,128]{2,1,0:T(8,128)S(1)}, u32[]{:S(2)}, u32[]{:S(2)}) %all-to-all-start.2) | async-done | bytes 262176 | tf_op jit(solution)/shard_map/all_to_all | solution.py:84
  78.3 1.4 fusion.27
  79.7 0.8 reshape.74
  80.5 3.4 %all-to-all-start.4 = ((f32[16,1,1024]{2,1,0:T(1,128)}), f32[16,1,1024]{2,1,0:T(1,128)S(1)}, u32[]{:S(2)}, u32[]{:S(2)}) async-start(f32[16,1,1024]{2,1,0:T(1,128)} %reshape.74), calls=%async_computation.4 | async-start | bytes 131072 | tf_op jit(solution)/shard_map/all_to_all | solution.py:43
  83.9 7.0 %all-to-all-done.4 = f32[16,1,1024]{2,1,0:T(1,128)S(1)} async-done(((f32[16,1,1024]{2,1,0:T(1,128)}), f32[16,1,1024]{2,1,0:T(1,128)S(1)}, u32[]{:S(2)}, u32[]{:S(2)}) %all-to-all-start.4) | async-done | bytes 65568 | tf_op jit(solution)/shard_map/all_to_all | solution.py:43
  91.0 0.9 broadcast_in_dim.47
  91.8 5.6 %all-to-all-start.3 = ((f32[32,32,128]{2,1,0:T(8,128)}), f32[32,32,128]{2,1,0:T(8,128)S(1)}, u32[]{:S(2)}, u32[]{:S(2)}) async-start(f32[32,32,128]{2,1,0:T(8,128)} %broadcast_in_dim.47), calls=%async_computation.3 | async-start | bytes 1048576 | tf_op jit(solution)/shard_map/all_to_all | solution.py:43
  99.3 0.8 reduce.6
  100.2 11.3 %all-to-all-done.3 = f32[32,32,128]{2,1,0:T(8,128)S(1)} async-done(((f32[32,32,128]{2,1,0:T(8,128)}), f32[32,32,128]{2,1,0:T(8,128)S(1)}, u32[]{:S(2)}, u32[]{:S(2)}) %all-to-all-start.3) | async-done | bytes 524320 | tf_op jit(solution)/shard_map/all_to_all | solution.py:43
  111.9 0.7 multiply_add_fusion
  112.8 2.8 %cholesky.59 = f32[31,31]{1,0:T(8,128)S(1)} custom-call(f32[31,31]{1,0:T(8,128)S(1)} %fusion.44), custom_call_target="Cholesky" | custom-call | tf_op jit(solution)/shard_map/jit(cholesky)/cholesky | solution.py:36
  115.7 0.7 compare_reduce_fusion.2
  117.0 2.4 %custom-call.9 = f32[1,31,31]{1,2,0:T(8,128)S(1)} custom-call(f32[1,31,31]{2,1,0:T(8,128)S(1)} %fusion.21), custom_call_target="InvertDiagBlocksLowerTriangular" | custom-call | tf_op jit(solution)/shard_map/jit(_cho_solve)/triangular_solve | solution.py:37
  121.0 4.0 %fusion.13 = f32[512,31]{0,1:T(8,128)S(1)} fusion(f32[1024,31]{0,1:T(8,128)S(1)} %convolution_subtract_fusion, f32[512,1024]{1,0:T(8,128)} %copy-done), kind=kOutput, calls=%fused_computation.25 | convolution fusion | flops 198180864 | bytes 2287616 | tf_op jit(solution)/shard_map/mn,nc->mc/dot_general | solution.py:15
  125.8 18.1 %all_to_all.46 = f32[16,32,128]{2,1,0:T(8,128)S(1)} all-to-all(f32[16,32,128]{2,1,0:T(8,128)S(1)} %broadcast_in_dim.49), channel_id=1, replica_groups=mesh['row'=32,'col'=16] {'col'}, dimensions={0} | all-to-all | bytes 524288 | tf_op jit(solution)/shard_map/all_to_all | solution.py:43
  144.0 0.9 broadcast_in_dim.50
  144.8 5.5 %all-to-all-start.6 = ((f32[32,32,128]{2,1,0:T(8,128)}), f32[32,32,128]{2,1,0:T(8,128)S(1)}, u32[]{:S(2)}, u32[]{:S(2)}) async-start(f32[32,32,128]{2,1,0:T(8,128)} %broadcast_in_dim.50), calls=%async_computation.6 | async-start | bytes 1048576 | tf_op jit(solution)/shard_map/all_to_all | solution.py:43
  150.5 0.8 copy.124
  151.5 2.8 %cholesky.70 = f32[31,31]{1,0:T(8,128)S(1)} custom-call(f32[31,31]{1,0:T(8,128)S(1)} %fusion.39), custom_call_target="Cholesky" | custom-call | tf_op jit(solution)/shard_map/jit(cholesky)/cholesky | solution.py:36
  154.3 0.7 compare_reduce_fusion.1
  155.0 0.7 fusion.22
  155.7 2.4 %custom-call.10 = f32[1,31,31]{1,2,0:T(8,128)S(1)} custom-call(f32[1,31,31]{2,1,0:T(8,128)S(1)} %fusion.22), custom_call_target="InvertDiagBlocksLowerTriangular" | custom-call | tf_op jit(solution)/shard_map/jit(_cho_solve)/triangular_solve | solution.py:37
  158.1 9.1 %all-to-all-done.6 = f32[32,32,128]{2,1,0:T(8,128)S(1)} async-done(((f32[32,32,128]{2,1,0:T(8,128)}), f32[32,32,128]{2,1,0:T(8,128)S(1)}, u32[]{:S(2)}, u32[]{:S(2)}) %all-to-all-start.6) | async-done | bytes 524320 | tf_op jit(solution)/shard_map/all_to_all | solution.py:43
  168.5 0.9 convolution_add_fusion.3
  169.6 2.8 %cholesky.81 = f32[31,31]{1,0:T(8,128)S(1)} custom-call(f32[31,31]{1,0:T(8,128)S(1)} %fusion.33), custom_call_target="Cholesky" | custom-call | tf_op jit(solution)/shard_map/jit(cholesky)/cholesky | solution.py:36
  172.4 0.7 compare_reduce_fusion
  173.7 2.4 %custom-call.11 = f32[1,31,31]{1,2,0:T(8,128)S(1)} custom-call(f32[1,31,31]{2,1,0:T(8,128)S(1)} %fusion.23), custom_call_target="InvertDiagBlocksLowerTriangular" | custom-call | tf_op jit(solution)/shard_map/jit(_cho_solve)/triangular_solve | solution.py:37
  177.4 0.7 fusion.55
  178.5 0.7 fusion.28
  180.7 5.8 %multiply_reduce_fusion = (f32[]{:T(128)}, f32[512,1024]{1,0:T(8,128)}) fusion(f32[512,1024]{1,0:T(8,128)} %copy-done, f32[512,31]{0,1:T(8,128)S(1)} %fusion.5, f32[1024,1]{0,1:T(1,128)S(1)} %bitcast.151, f32[1024,30]{0,1:T(8,128)S(1)} %copy-done.1), kind=kOutput, calls=%fused_computation | convolution fusion | flops 199261184 | bytes 4384772 | tf_op jit(solution)/shard_map/mc,nc->mn/dot_general | solution.py:15
  187.8 5.2 %fusion = f32[512,129]{0,1:T(8,128)S(1)} fusion(f32[512,1024]{1,0:T(8,128)} %get-tuple-element.28, f32[512,1024]{1,0:T(8,128)} %copy-done, f32[1024,64]{1,0:T(8,128)S(1)} %get-tuple-element.17, f32[1024,64]{1,0:T(8,128)S(1)} %get-tuple-element.16, f32[129]{0:T(256)S(1)} %pad.40.clone), kind=kOutput, calls=%fused_computation.1 | convolution fusion | flops 814483456 | bytes 4983300 | tf_op jit(solution)/shard_map/mn,nf->mf/dot_general | solution.py:15
  193.8 10.0 %all_to_all.47 = f32[16,1,128]{2,1,0:T(1,128)S(1)} all-to-all(f32[16,1,128]{2,1,0:T(1,128)S(1)} %broadcast_in_dim.104), channel_id=1, replica_groups=mesh['row'=32,'col'=16] {'col'}, dimensions={0} | all-to-all | bytes 16384 | tf_op jit(solution)/shard_map/all_to_all | solution.py:43
  204.5 5.7 %all-to-all-start.8 = ((f32[32,1,128]{2,1,0:T(1,128)}), f32[32,1,128]{2,1,0:T(1,128)S(1)}, u32[]{:S(2)}, u32[]{:S(2)}) async-start(f32[32,1,128]{2,1,0:T(1,128)} %broadcast_in_dim.105), calls=%async_computation.8 | async-start | bytes 32768 | tf_op jit(solution)/shard_map/all_to_all | solution.py:43
  210.1 0.7 copy.127
  210.8 7.9 %all-to-all-done.8 = f32[32,1,128]{2,1,0:T(1,128)S(1)} async-done(((f32[32,1,128]{2,1,0:T(1,128)}), f32[32,1,128]{2,1,0:T(1,128)S(1)}, u32[]{:S(2)}, u32[]{:S(2)}) %all-to-all-start.8) | async-done | bytes 16416 | tf_op jit(solution)/shard_map/all_to_all | solution.py:43
  (94 shorter events, 13.4 us)
Async XLA Ops:
  27.3 26.2 %all-to-all-start.1 = ((f32[32,32,128]{2,1,0:T(8,128)}), f32[32,32,128]{2,1,0:T(8,128)S(1)}, u32[]{:S(2)}, u32[]{:S(2)}) async-start(f32[32,32,128]{2,1,0:T(8,128)} %broadcast_in_dim.44), calls=%async_computation.1 | async-start | bytes 1048576 | tf_op jit(solution)/shard_map/all_to_all | solution.py:43
  56.3 1.4 copy-start
  60.1 6.2 %copy-start.2 = (f32[2]{0:T(128)S(1)}, f32[2]{0:T(128)}, u32[]{:S(2)}) copy-start(f32[2]{0:T(128)} %param.10) | copy-start | bytes 28
  62.0 16.2 %all-to-all-start.2 = ((f32[16,32,128]{2,1,0:T(8,128)}), f32[16,32,128]{2,1,0:T(8,128)S(1)}, u32[]{:S(2)}, u32[]{:S(2)}) async-start(f32[16,32,128]{2,1,0:T(8,128)} %maximum_maximum_fusion), calls=%async_computation.2 | async-start | bytes 524288 | tf_op jit(solution)/shard_map/all_to_all | solution.py:84
  80.5 10.5 %all-to-all-start.4 = ((f32[16,1,1024]{2,1,0:T(1,128)}), f32[16,1,1024]{2,1,0:T(1,128)S(1)}, u32[]{:S(2)}, u32[]{:S(2)}) async-start(f32[16,1,1024]{2,1,0:T(1,128)} %reshape.74), calls=%async_computation.4 | async-start | bytes 131072 | tf_op jit(solution)/shard_map/all_to_all | solution.py:43
  91.8 19.6 %all-to-all-start.3 = ((f32[32,32,128]{2,1,0:T(8,128)}), f32[32,32,128]{2,1,0:T(8,128)S(1)}, u32[]{:S(2)}, u32[]{:S(2)}) async-start(f32[32,32,128]{2,1,0:T(8,128)} %broadcast_in_dim.47), calls=%async_computation.3 | async-start | bytes 1048576 | tf_op jit(solution)/shard_map/all_to_all | solution.py:43
  144.8 22.4 %all-to-all-start.6 = ((f32[32,32,128]{2,1,0:T(8,128)}), f32[32,32,128]{2,1,0:T(8,128)S(1)}, u32[]{:S(2)}, u32[]{:S(2)}) async-start(f32[32,32,128]{2,1,0:T(8,128)} %broadcast_in_dim.50), calls=%async_computation.6 | async-start | bytes 1048576 | tf_op jit(solution)/shard_map/all_to_all | solution.py:43
  151.4 29.3 %copy-start.1 = (f32[1024,30]{0,1:T(8,128)S(1)}, f32[1024,30]{0,1:T(8,128)}, u32[]{:S(2)}) copy-start(f32[1024,30]{0,1:T(8,128)} %copy.124) | copy-start | bytes 368644
  204.5 14.3 %all-to-all-start.8 = ((f32[32,1,128]{2,1,0:T(1,128)}), f32[32,1,128]{2,1,0:T(1,128)S(1)}, u32[]{:S(2)}, u32[]{:S(2)}) async-start(f32[32,1,128]{2,1,0:T(1,128)} %broadcast_in_dim.105), calls=%async_computation.8 | async-start | bytes 32768 | tf_op jit(solution)/shard_map/all_to_all | solution.py:43

commit v2 on v1

v2 whole, which is shorter than its diff:
```python
import functools

import jax
import jax.numpy as jnp
from jax import lax
from jax.experimental import pallas as pl
from jax.experimental.pallas import tpu as pltpu
from jax.sharding import PartitionSpec as P

PROBES = 30
COLS = 31
FEAT = 64
PAD = 32
f32 = jnp.float32
highest = lax.Precision.HIGHEST
PARAMS = pltpu.CompilerParams(vmem_limit_bytes=48 * 1024 * 1024)


def dot(left, right, left_dim=1, right_dim=0):
    return lax.dot_general(
        left, right, (((left_dim,), (right_dim,)), ((), ())), precision=highest, preferred_element_type=f32
    )


def pack(square):
    return jnp.concatenate([square[8 * g : 8 * g + 8] for g in range(4)], 1)


def unpack(rows):
    return jnp.concatenate([rows[:, PAD * g : PAD * g + PAD] for g in range(4)], 0)


def unpack_columns(ref, start):
    count = ref.shape[0]
    pieces = [ref[:, start : start + 8, PAD * g : PAD * g + PAD].reshape(8 * count, PAD) for g in range(4)]
    return jnp.concatenate(pieces, 0)


def unpack_points(ref):
    count = ref.shape[0]
    pieces = []
    for g in range(4):
        top, left = 8 * (g // 2), FEAT * (g % 2)
        pieces.append(ref[:, top : top + 8, left : left + FEAT].reshape(8 * count, FEAT))
    return jnp.concatenate(pieces, 0)


def places(rows=PAD, columns=PAD):
    shape = (rows, columns)
    return lax.broadcasted_iota(jnp.int32, shape, 0), lax.broadcasted_iota(jnp.int32, shape, 1)


def symmetric(matrix):
    return 0.5 * (matrix + matrix.T)


def join_symmetric(first, second):
    down, across = places()
    diagonal = jnp.sum(jnp.where(down == across, second, 0.0), 0, keepdims=True)
    return jnp.where(down == PAD - 1, diagonal, jnp.where(down >= across, first, second))


def part_symmetric(joined):
    down, across = places()
    inside = down < PAD - 1
    lower = jnp.where((down >= across) & inside, joined, 0.0)
    upper = jnp.where(down < across, joined, 0.0)
    eye = down == across
    first = jnp.where(eye, lower, lower + lower.T)
    second = upper + upper.T + jnp.where(eye, joined[PAD - 1 : PAD, :], 0.0)
    return first, second


def eliminate(systems):
    down = lax.broadcasted_iota(jnp.int32, (PAD, 1), 0)
    for k in range(COLS):
        for n, system in enumerate(systems):
            row = system[k : k + 1, :] * (1.0 / system[k : k + 1, k : k + 1])
            column = jnp.where(down == k, 0.0, system[:, k : k + 1])
            kept = jnp.where(down == k, row, system)
            systems[n] = kept - column * row
    return [system[:, PAD:] for system in systems]


def identity():
    down, across = places()
    return jnp.where(down == across, 1.0, 0.0)


def start_kernel(points_ref, lengths_ref, probes_ref, targets_ref, row_ref, col_ref):
    scaled = points_ref[...] / lengths_ref[...]
    rhs = jnp.concatenate([probes_ref[...], targets_ref[...], jnp.zeros((1, PAD), f32)], 0).T
    pairs = [jnp.concatenate([scaled[16 * g : 16 * g + 8], scaled[16 * g + 8 : 16 * g + 16]], 1) for g in range(2)]
    block = jnp.concatenate(pairs + [pack(rhs)], 0)
    row_ref[...] = jnp.broadcast_to(block[None], row_ref.shape)
    col_ref[...] = jnp.broadcast_to(block[None], col_ref.shape)


def augmented(points, last, one):
    norm = jnp.sum(points * points, 1, keepdims=True)
    across = lax.broadcasted_iota(jnp.int32, (points.shape[0], FEAT), 1)
    tail = jnp.where(across == last, norm, jnp.where(across == one, 1.0, 0.0))
    return jnp.concatenate([points, tail], 1)


def tile_kernel(row_ref, col_ref, own_ref, base_ref, slope_ref, message_ref):
    row_points = unpack_points(row_ref)
    col_points = unpack_points(col_ref)
    left = augmented(row_points, 0, 1)
    right = augmented(col_points, 1, 0)
    across = lax.broadcasted_iota(jnp.int32, right.shape, 1)
    right = jnp.where(across < FEAT, -10.0 * right, 5.0 * right)
    base_ref[...] = dot(left, right, 1, 1)

    def strip(i, carry):
        here = pl.ds(pl.multiple_of(i * 16, 16), 16)
        squared = jnp.maximum(base_ref[here, :], 0.0)
        dist = squared * lax.rsqrt(jnp.maximum(squared, 1e-30))
        decayed = jnp.exp(-dist)
        more = 1.0 + dist
        slope_ref[here, :] = more * decayed
        base_ref[here, :] = (more + squared * (1.0 / 3.0)) * decayed
        return carry

    lax.fori_loop(0, base_ref.shape[0] // 16, strip, 0)
    row_rhs = unpack_columns(row_ref, 16)
    col_rhs = unpack_columns(col_ref, 16)
    own_rhs = unpack(own_ref[16:24, :])
    partial = dot(base_ref[...], col_rhs)
    curvature = dot(row_rhs, partial, 0, 0)
    gram = dot(own_rhs, own_rhs, 0, 0)
    quarter = partial.shape[0] // 4
    chunks = jnp.concatenate([partial[quarter * g : quarter * g + quarter] for g in range(4)], 1)
    message_ref[:, 0:8, :] = chunks.reshape(quarter // 8, 8, 128)
    grams = pack(join_symmetric(symmetric(curvature), gram))
    message_ref[:, 8:16, :] = jnp.broadcast_to(grams[None], (quarter // 8, 8, 128))


def images_kernel(variances_ref, got_ref, own_ref, row_ref, col_ref):
    summed = jnp.sum(got_ref[...], 0)
    images = variances_ref[0] * summed[0:8] + variances_ref[1] * own_ref[16:24, :]
    row_ref[...] = jnp.broadcast_to(images[None], row_ref.shape)
    col_ref[...] = jnp.broadcast_to(jnp.concatenate([images, summed[8:16]], 0)[None], col_ref.shape)


def advance_kernel(variances_ref, got_ref, col_ref, base_ref, advance_ref, inverse_ref, curvature_ref, res_ref, product_ref):
    base_curvature, res_gram = part_symmetric(unpack(jnp.sum(got_ref[:, 8:16, :], 0)))
    curvature = variances_ref[0] * base_curvature + variances_ref[1] * res_gram
    advance, inverse = eliminate(
        [jnp.concatenate([curvature, res_gram], 1), jnp.concatenate([res_gram, identity()], 1)]
    )
    residual = unpack_columns(col_ref, 16) - dot(unpack_columns(got_ref, 0), advance)
    res_ref[...] = residual
    advance_ref[...] = advance
    inverse_ref[...] = inverse
    curvature_ref[...] = curvature
    product_ref[...] = dot(base_ref[...], residual)


def grams_kernel(got_ref, row_ref, own_ref, images_ref, advance_ref, product_ref, res_ref, own_res_ref, message_ref):
    advance = advance_ref[...]
    residual = unpack_columns(row_ref, 16) - dot(unpack_columns(got_ref, 0), advance)
    res_ref[...] = residual
    own_res = unpack(own_ref[16:24, :]) - dot(unpack(images_ref[0]), advance)
    own_res_ref[...] = own_res
    curvature = dot(residual, product_ref[...], 0, 0)
    gram = dot(own_res, own_res, 0, 0)
    message = pack(join_symmetric(symmetric(curvature), gram))
    message_ref[...] = jnp.broadcast_to(message[None], message_ref.shape)


def gradient_kernel(
    total_points,
    variances_ref,
    got_ref,
    advance_ref,
    inverse_ref,
    curvature_ref,
    row_ref,
    col_ref,
    own_ref,
    row_res_ref,
    col_res_ref,
    own_res_ref,
    base_ref,
    slope_ref,
    solves_ref,
    terms_ref,
    matrix_ref,
):
    signal_var, noise_var = variances_ref[0], variances_ref[1]
    base_curvature, next_gram = part_symmetric(unpack(jnp.sum(got_ref[...], 0)))
    carry_over = dot(inverse_ref[...], next_gram)
    next_curv = (
        signal_var * base_curvature
        + noise_var * next_gram
        - symmetric(dot(carry_over, dot(curvature_ref[...], carry_over), 0, 0))
    )
    (next_advance,) = eliminate([jnp.concatenate([next_curv, next_gram], 1)])
    rhs_coef = advance_ref[...] + dot(carry_over, next_advance)

    def solves_of(rhs, residual):
        return dot(rhs, rhs_coef) + dot(residual, next_advance)

    def pair_of(rhs, solves):
        across = lax.broadcasted_iota(jnp.int32, rhs.shape, 1)
        return jnp.where(across < PROBES, rhs, solves)

    own_rhs = unpack(own_ref[16:24, :])
    own_solves = solves_of(own_rhs, own_res_ref[...])
    solves_ref[...] = own_solves.T[0:COLS, :]
    col_rhs = unpack_columns(col_ref, 16)
    col_pair = pair_of(col_rhs, solves_of(col_rhs, col_res_ref[...]))
    across = lax.broadcasted_iota(jnp.int32, (1, PAD), 1)
    weights = jnp.where(across < PROBES, -1.0 / PROBES, 1.0) * (0.5 / total_points)
    row_weights = solves_of(unpack_columns(row_ref, 16), row_res_ref[...]) * weights
    matrix_ref[...] = dot(row_weights, col_pair, 1, 1)

    def strip(i, total):
        here = pl.ds(pl.multiple_of(i * 16, 16), 16)
        values = matrix_ref[here, :]
        matrix_ref[here, :] = values * slope_ref[here, :]
        return total + values * base_ref[here, :]

    signal = lax.fori_loop(0, matrix_ref.shape[0] // 16, strip, jnp.zeros((16, matrix_ref.shape[1]), f32))
    row_points = unpack_points(row_ref)
    col_points = unpack_points(col_ref)
    right = jnp.concatenate([col_points, col_points * col_points, jnp.ones((col_points.shape[0], 128), f32)], 1)
    moved = dot(matrix_ref[...], right)
    scales = row_points * (row_points * moved[:, 128 : 128 + FEAT] - 2.0 * moved[:, :FEAT]) + moved[:, FEAT:128]
    scale_terms = (5.0 / 3.0 * signal_var) * jnp.sum(scales, 0, keepdims=True)
    signal_term = signal_var * jnp.sum(jnp.sum(signal, 0, keepdims=True), 1, keepdims=True)
    noise = jnp.sum(own_solves * weights * pair_of(own_rhs, own_solves), 0, keepdims=True)
    noise_term = noise_var * jnp.sum(noise, 1, keepdims=True)
    terms_ref[...] = jnp.concatenate([scale_terms, signal_term, noise_term, jnp.zeros((1, FEAT - 2), f32)], 1)


def shape_of(*dims):
    return jax.ShapeDtypeStruct(dims, f32)


def call(kernel, outs, *operands, scalars=0, scratch=(), flops=1):
    smem = [pl.BlockSpec(memory_space=pltpu.SMEM)] * scalars
    vmem = [pl.BlockSpec(memory_space=pltpu.VMEM)] * (len(operands) - scalars)
    return pl.pallas_call(
        kernel,
        out_shape=outs,
        in_specs=smem + vmem,
        out_specs=[pl.BlockSpec(memory_space=pltpu.VMEM)] * len(outs),
        scratch_shapes=scratch,
        compiler_params=PARAMS,
        cost_estimate=pl.CostEstimate(flops=flops, bytes_accessed=1 << 20, transcendentals=0),
    )(*operands)


def exchange(blocks, axis):
    return lax.all_to_all(blocks, axis, 0, 0, tiled=True)


def local(points, length_scales, variances, targets, probe_vectors):
    rows = lax.axis_size("row")
    cols = lax.axis_size("col")
    width = points.shape[1]
    row_block, col_set = cols * width, rows * width
    total_points = width * rows * cols
    to_row, to_col = call(
        start_kernel,
        [shape_of(cols, 24, 128), shape_of(rows, 24, 128)],
        points.T,
        length_scales[None],
        probe_vectors,
        targets[None],
    )
    own = to_row[0]
    row_got = exchange(to_row, "col")
    col_got = exchange(to_col, "row")
    base, slope, message = call(
        tile_kernel,
        [shape_of(row_block, col_set), shape_of(row_block, col_set), shape_of(cols, 16, 128)],
        row_got,
        col_got,
        own,
    )
    images_row, images_col = call(
        images_kernel,
        [shape_of(cols, 8, 128), shape_of(rows, 16, 128)],
        variances,
        exchange(message, "col"),
        own,
        scalars=1,
    )
    images_col_got = exchange(images_col, "row")
    images_row_got = exchange(images_row, "col")
    square = shape_of(PAD, PAD)
    advance, inverse, curvature, col_res, product = call(
        advance_kernel,
        [square, square, square, shape_of(col_set, PAD), shape_of(row_block, PAD)],
        variances,
        images_col_got,
        col_got,
        base,
        scalars=1,
    )
    row_res, own_res, message = call(
        grams_kernel,
        [shape_of(row_block, PAD), square, shape_of(cols, 8, 128)],
        images_row_got,
        row_got,
        own,
        images_row,
        advance,
        product,
    )
    summed = jnp.sum(exchange(message, "col"), 0)
    grams_got = exchange(jnp.broadcast_to(summed[None], (rows, 8, 128)), "row")
    solves, terms = call(
        functools.partial(gradient_kernel, total_points),
        [shape_of(COLS, width), shape_of(1, 128)],
        variances,
        grams_got,
        advance,
        inverse,
        curvature,
        row_got,
        col_got,
        own,
        row_res,
        col_res,
        own_res,
        base,
        slope,
        scalars=1,
        scratch=[pltpu.VMEM((row_block, col_set), f32)],
    )
    terms = jnp.sum(exchange(jnp.broadcast_to(terms[None], (cols, 1, 128)), "col"), 0)
    terms = jnp.sum(exchange(jnp.broadcast_to(terms[None], (rows, 1, 128)), "row"), 0)
    return (solves, terms[0, : FEAT + 2])


def solution(mesh):
    placed = (P(None, ("row", "col")), P(), P(), P(("row", "col")), P(None, ("row", "col")))
    return jax.shard_map(
        local, mesh=mesh, in_specs=placed, out_specs=(P(None, ("row", "col")), P()), check_vma=False
    )
```

time: 220 us -> 181 us (0.82)
  blocking collectives: 51.5 us -> 104 us
  waiting for transfers between devices: 62.6 us -> 13.2 us
  Pallas kernels: 0 us -> 32.7 us
  matrix products: 27.5 us -> 0 us
  other arithmetic: 26.6 us -> 0.65 us
  starting transfers between devices: 34.1 us -> 14.6 us
  between operations: 4.27 us -> 0.72 us
    all_to_all x3 -> x7, blocking collectives: 51.5 us -> 104 us  [exchange(): return lax.all_to_all(blocks, axis, 0, 0, tiled=True)]
    all_to_all x6 -> x2, waiting for transfers between devices: 62.6 us -> 13.2 us  [exchange(): return lax.all_to_all(blocks, axis, 0, 0, tiled=True)]
    pallas_call x0 -> x6, Pallas kernels: none -> 32.7 us  [call(): pl.pallas_call(kernel, out_shape=outs, in_specs=smem + vmem, out_specs=[p...]
    dot_general x23 -> x0, matrix products: 26.2 us -> none  [mul(): jnp.einsum(spec, left, right, precision=highest, preferred_element_type=j...]
    another operation x15 -> x0, other arithmetic: 19.6 us -> none  [the longest x9 10.6 us: solve_spd(): lower = jnp.linalg.cholesky(matrix)]
    all_to_all x6 -> x2, starting transfers between devices: 34.1 us -> 14.6 us  [exchange(): return lax.all_to_all(blocks, axis, 0, 0, tiled=True)]
    unnamed x18 -> x36, local copies, waits for them, and re-layouts: 4.82 us -> 13.3 us
    broadcast_in_dim x13 -> x3, local copies, waits for them, and re-layouts: 4.02 us -> 0.71 us  [the longest x1 0.69 us: local(): grams_got = exchange(jnp.broadcast_to(summed[None], (rows, 8, 128)), 'row')]
  transfers between devices with their start and end apart: 6 -> 2, of which waited for: 6 -> 1; matrix products, arithmetic and copies ran while one was open for 5% -> 0% of each run, Pallas kernels for 0% -> 4%
where the time goes in v2:
time: 181 us; the launch traced here: 180 us
  blocking collectives  104 us (57%)
  Pallas kernels  32.7 us (18%)
  starting transfers between devices  14.6 us (8%)
  local copies, waits for them, and re-layouts  14.5 us (8%)
  waiting for transfers between devices  13.2 us (7%)
    all_to_all x7, blocking collectives, exchange(): return lax.all_to_all(blocks, axis, 0, 0, tiled=True)  104 us
    pallas_call x6, Pallas kernels, call(): pl.pallas_call(kernel, out_shape=outs, in_specs=smem + vmem, out_specs=[p...  32.7 us
    all_to_all x2, starting transfers between devices, exchange(): return lax.all_to_all(blocks, axis, 0, 0, tiled=True)  14.6 us
    unnamed x36, local copies, waits for them, and re-layouts  13.3 us
    all_to_all x2, waiting for transfers between devices, exchange(): return lax.all_to_all(blocks, axis, 0, 0, tiled=True)  13.2 us
  transfers between devices with their start and end apart: 2, of which 1 were waited for; matrix products, arithmetic and copies ran while one was open for 0% of the time, Pallas kernels for 4%

profile of v2, /device:TPU:1, one launch (start us, length us, event | category | flops | bytes accessed | tf_op | source)
XLA Modules:
  0.0 180.0 jit_solution(2726508765373190073)
XLA Ops:
  0.6 0.0 copy-start.15
  0.6 0.0 copy-start.7
  0.7 0.7 copy-done.7
  1.4 0.0 copy-start.8
  1.4 0.7 copy-done.8
  2.1 0.0 copy-start.16
  2.1 0.7 copy-done.16
  2.7 0.0 copy-start.17
  2.7 0.7 copy-done.17
  3.4 0.9 shard_map.68
  4.3 21.9 %all_to_all.45.row_ref = f32[16,24,128]{2,1,0:T(8,128)S(1)} all-to-all(f32[16,24,128]{2,1,0:T(8,128)S(1)} %get-tuple-element.19), channel_id=1, replica_groups=mesh['row'=32,'col'=16] {'col'}, dimensions={0} | all-to-all | bytes 393216 | tf_op jit(solution)/shard_map/all_to_all | solution.py:257
  26.2 9.7 %all-to-all-start.1 = ((f32[32,24,128]{2,1,0:T(8,128)}), f32[32,24,128]{2,1,0:T(8,128)S(1)}, u32[]{:S(2)}, u32[]{:S(2)}) async-start(f32[32,24,128]{2,1,0:T(8,128)} %get-tuple-element.20), calls=%async_computation.1 | async-start | bytes 786432 | tf_op jit(solution)/shard_map/all_to_all | solution.py:257
  35.9 13.2 %all-to-all-done.1.col_ref = f32[32,24,128]{2,1,0:T(8,128)S(1)} async-done(((f32[32,24,128]{2,1,0:T(8,128)}), f32[32,24,128]{2,1,0:T(8,128)S(1)}, u32[]{:S(2)}, u32[]{:S(2)}) %all-to-all-start.1) | async-done | bytes 393248 | tf_op jit(solution)/shard_map/all_to_all | solution.py:257
  49.1 9.1 %shard_map.69 = (f32[512,1024]{1,0:T(8,128)S(1)}, f32[512,1024]{1,0:T(8,128)S(1)}, f32[16,16,128]{2,1,0:T(8,128)S(1)}) custom-call(f32[16,24,128]{2,1,0:T(8,128)S(1)} %all_to_all.45.row_ref, f32[32,24,128]{2,1,0:T(8,128)S(1)} %all-to-all-done.1.col_ref, f32[24,128]{1,0:T(8,128)S(1)} %slice_bitcast_fusion.own_ref), custom_call_target="tpu_custom_call" | custom-call | flops 1 | bytes 1048576 | tf_op jit(solution)/shard_map/pallas_call | solution.py:245
  58.2 0.0 copy-start
  58.2 1.3 copy-done
  59.5 13.5 %all_to_all.46.got_ref = f32[16,16,128]{2,1,0:T(8,128)S(1)} all-to-all(f32[16,16,128]{2,1,0:T(8,128)S(1)} %get-tuple-element.21), channel_id=1, replica_groups=mesh['row'=32,'col'=16] {'col'}, dimensions={0} | all-to-all | bytes 262144 | tf_op jit(solution)/shard_map/all_to_all | solution.py:257
  73.0 0.0 copy-done.15
  73.0 1.2 shard_map.70
  74.2 15.8 %all_to_all.47.got_ref = f32[32,16,128]{2,1,0:T(8,128)S(1)} all-to-all(f32[32,16,128]{2,1,0:T(8,128)S(1)} %get-tuple-element.23), channel_id=1, replica_groups=mesh['row'=32,'col'=16] {'row'}, dimensions={0} | all-to-all | bytes 524288 | tf_op jit(solution)/shard_map/all_to_all | solution.py:257
  90.0 5.0 %all-to-all-start.3 = ((f32[16,8,128]{2,1,0:T(8,128)}), f32[16,8,128]{2,1,0:T(8,128)S(1)}, u32[]{:S(2)}, u32[]{:S(2)}) async-start(f32[16,8,128]{2,1,0:T(8,128)} %get-tuple-element.22.images_ref), calls=%async_computation.3 | async-start | bytes 131072 | tf_op jit(solution)/shard_map/all_to_all | solution.py:257
  95.0 6.5 %shard_map.71 = (f32[32,32]{1,0:T(8,128)S(1)}, f32[32,32]{1,0:T(8,128)S(1)}, f32[32,32]{1,0:T(8,128)S(1)}, f32[1024,32]{1,0:T(8,128)S(1)}, f32[512,32]{1,0:T(8,128)S(1)}) custom-call(f32[2]{0:T(128)S(1)} %copy-done.15, f32[32,16,128]{2,1,0:T(8,128)S(1)} %all_to_all.47.got_ref, f32[32,24,128]{2,1,0:T(8,128)S(1)} %all-to-all-done.1.col_ref, ...), custom_call_target="tpu_custom_call" | custom-call | flops 1 | bytes 1048576 | tf_op jit(solution)/shard_map/pallas_call | solution.py:245
  101.5 0.0 copy-start.2
  101.5 0.7 copy-done.2
  102.2 0.0 copy-start.4
  102.2 0.6 copy-done.4
  102.8 0.0 copy-start.9
  102.8 0.6 copy-done.9
  103.4 0.0 copy-start.11
  103.4 0.6 copy-done.11
  104.0 0.0 all-to-all-done.3.got_ref
  104.0 0.9 copy-done.3
  104.9 0.7 copy-done.5
  105.6 1.9 %shard_map.72 = (f32[512,32]{1,0:T(8,128)S(1)}, f32[32,32]{1,0:T(8,128)S(1)}, f32[16,8,128]{2,1,0:T(8,128)S(1)}) custom-call(f32[16,8,128]{2,1,0:T(8,128)S(1)} %all-to-all-done.3.got_ref, f32[16,24,128]{2,1,0:T(8,128)S(1)} %all_to_all.45.row_ref, f32[24,128]{1,0:T(8,128)S(1)} %slice_bitcast_fusion.own_ref, f32[16,8,128]{2,1,0:T(8,128)} %get-tuple-element.22.images_ref, ...), custom_call_target="tpu_custom_call" | custom-call | flops 1 | bytes 1048576 | tf_op jit(solution)/shard_map/pallas_call | solution.py:245
  107.5 0.6 copy-done.13
  108.1 14.9 %all_to_all.48 = f32[16,8,128]{2,1,0:T(8,128)S(1)} all-to-all(f32[16,8,128]{2,1,0:T(8,128)S(1)} %get-tuple-element.27), channel_id=1, replica_groups=mesh['row'=32,'col'=16] {'col'}, dimensions={0} | all-to-all | bytes 131072 | tf_op jit(solution)/shard_map/all_to_all | solution.py:257
  123.0 0.6 reduce_sum.29
  123.6 0.7 broadcast_in_dim.28
  124.3 14.1 %all_to_all.49.got_ref = f32[32,8,128]{2,1,0:T(8,128)S(1)} all-to-all(f32[32,8,128]{2,1,0:T(8,128)S(1)} %broadcast_in_dim.28), channel_id=1, replica_groups=mesh['row'=32,'col'=16] {'row'}, dimensions={0} | all-to-all | bytes 262144 | tf_op jit(solution)/shard_map/all_to_all | solution.py:257
  138.3 1.6 copy-done.1
  139.9 0.7 copy-done.6
  140.7 0.7 copy-done.10
  141.4 0.7 copy-done.12
  142.1 0.7 copy-done.14
  142.8 13.1 %shard_map.73 = (f32[31,32]{1,0:T(8,128)}, f32[1,128]{1,0:T(1,128)S(1)}) custom-call(f32[2]{0:T(128)S(1)} %copy-done.15, f32[32,8,128]{2,1,0:T(8,128)S(1)} %all_to_all.49.got_ref, f32[32,32]{1,0:T(8,128)S(1)} %copy-done.6, f32[32,32]{1,0:T(8,128)S(1)} %copy-done.10, f32[32,32]{1,0:T(8,128)S(1)} %copy-done.12, f32[16,24,128]{2,1,0:T(8,128)S(1)} %all_to_all.45.row_ref, ...), custom_call_target="tpu_custom_call" | custom-call | flops 1 | bytes 1048576 | tf_op jit(solution)/shard_map/pallas_call | solution.py:245
  156.0 11.5 %all_to_all.50 = f32[16,1,128]{2,1,0:T(1,128)S(1)} all-to-all(f32[16,1,128]{2,1,0:T(1,128)S(1)} %broadcast_in_dim.30), channel_id=1, replica_groups=mesh['row'=32,'col'=16] {'col'}, dimensions={0} | all-to-all | bytes 16384 | tf_op jit(solution)/shard_map/all_to_all | solution.py:257
  167.5 11.9 %all_to_all.51 = f32[32,1,128]{2,1,0:T(1,128)S(1)} all-to-all(f32[32,1,128]{2,1,0:T(1,128)S(1)} %broadcast_in_dim.31), channel_id=1, replica_groups=mesh['row'=32,'col'=16] {'row'}, dimensions={0} | all-to-all | bytes 32768 | tf_op jit(solution)/shard_map/all_to_all | solution.py:257
  179.4 0.5 slice_bitcast_fusion.1
  (13 shorter events, 0.1 us)
Async XLA Ops:
  0.6 72.4 %copy-start.15 = (f32[2]{0:T(128)S(1)}, f32[2]{0:T(128)}, u32[]{:S(2)}) copy-start(f32[2]{0:T(128)} %variances_ref.5) | copy-start | bytes 28
  0.6 0.7 copy-start.7
  1.4 0.7 copy-start.8
  2.1 0.7 copy-start.16
  2.7 0.7 copy-start.17
  26.2 22.8 %all-to-all-start.1 = ((f32[32,24,128]{2,1,0:T(8,128)}), f32[32,24,128]{2,1,0:T(8,128)S(1)}, u32[]{:S(2)}, u32[]{:S(2)}) async-start(f32[32,24,128]{2,1,0:T(8,128)} %get-tuple-element.20), calls=%async_computation.1 | async-start | bytes 786432 | tf_op jit(solution)/shard_map/all_to_all | solution.py:257
  58.2 1.4 copy-start
  90.0 14.0 %all-to-all-start.3 = ((f32[16,8,128]{2,1,0:T(8,128)}), f32[16,8,128]{2,1,0:T(8,128)S(1)}, u32[]{:S(2)}, u32[]{:S(2)}) async-start(f32[16,8,128]{2,1,0:T(8,128)} %get-tuple-element.22.images_ref), calls=%async_computation.3 | async-start | bytes 131072 | tf_op jit(solution)/shard_map/all_to_all | solution.py:257
  101.5 0.7 copy-start.2
  102.2 0.6 copy-start.4
  102.8 0.6 copy-start.9
  103.4 0.6 copy-start.11
  104.0 1.0 copy-start.3
  104.9 0.7 copy-start.5
  107.5 0.6 copy-start.13
  138.3 1.6 copy-start.1
  139.9 0.7 copy-start.6
  140.6 0.7 copy-start.10
  141.4 0.7 copy-start.12
  142.1 0.7 copy-start.14

commit v3 on v2

v3 whole, which is shorter than its diff:
```python
import functools

import jax
import jax.numpy as jnp
from jax import lax
from jax.experimental import pallas as pl
from jax.experimental.pallas import tpu as pltpu
from jax.sharding import PartitionSpec as P

PROBES = 30
COLS = 31
FEAT = 64
PAD = 32
f32 = jnp.float32
bf16 = jnp.bfloat16
root_five = 5.0**0.5
highest = lax.Precision.HIGHEST
PARAMS = pltpu.CompilerParams(vmem_limit_bytes=32 * 1024 * 1024)


def dot(left, right, left_dim=1, right_dim=0):
    return lax.dot_general(
        left, right, (((left_dim,), (right_dim,)), ((), ())), precision=highest, preferred_element_type=f32
    )


def pack(square):
    return jnp.concatenate([square[8 * g : 8 * g + 8] for g in range(4)], 1)


def unpack(rows):
    return jnp.concatenate([rows[:, PAD * g : PAD * g + PAD] for g in range(4)], 0)


def unpack_columns(ref, start):
    count = ref.shape[0]
    pieces = [ref[:, start : start + 8, PAD * g : PAD * g + PAD].reshape(8 * count, PAD) for g in range(4)]
    return jnp.concatenate(pieces, 0)


def unpack_points(ref):
    count = ref.shape[0]
    pieces = []
    for g in range(4):
        top, left = 8 * (g // 2), FEAT * (g % 2)
        pieces.append(ref[:, top : top + 8, left : left + FEAT].reshape(8 * count, FEAT))
    return jnp.concatenate(pieces, 0)


def places(rows=PAD, columns=PAD):
    shape = (rows, columns)
    return lax.broadcasted_iota(jnp.int32, shape, 0), lax.broadcasted_iota(jnp.int32, shape, 1)


def symmetric(matrix):
    return 0.5 * (matrix + matrix.T)


def join_symmetric(first, second):
    down, across = places()
    diagonal = jnp.sum(jnp.where(down == across, second, 0.0), 0, keepdims=True)
    return jnp.where(down == PAD - 1, diagonal, jnp.where(down >= across, first, second))


def part_symmetric(joined):
    down, across = places()
    inside = down < PAD - 1
    lower = jnp.where((down >= across) & inside, joined, 0.0)
    upper = jnp.where(down < across, joined, 0.0)
    eye = down == across
    first = jnp.where(eye, lower, lower + lower.T)
    second = upper + upper.T + jnp.where(eye, joined[PAD - 1 : PAD, :], 0.0)
    return first, second


def eliminate(systems):
    down = lax.broadcasted_iota(jnp.int32, (PAD, 1), 0)
    for k in range(COLS):
        for n, system in enumerate(systems):
            row = system[k : k + 1, :] * (1.0 / system[k : k + 1, k : k + 1])
            column = jnp.where(down == k, 0.0, system[:, k : k + 1])
            kept = jnp.where(down == k, row, system)
            systems[n] = kept - column * row
    return [system[:, PAD:] for system in systems]


def identity():
    down, across = places()
    return jnp.where(down == across, 1.0, 0.0)


def pieces_of(array, count=3):
    pieces = []
    for _ in range(count):
        piece = array.astype(bf16)
        pieces.append(piece)
        array = array - piece.astype(f32)
    return pieces


def bdot(left, right, right_dim=0):
    return lax.dot_general(left, right, (((1,), (right_dim,)), ((), ())), preferred_element_type=f32)


def left_pieces(array):
    high, mid, low = pieces_of(array)
    return jnp.concatenate([high, high, high, mid, mid, low], 1)


def right_pieces(array, dim):
    high, mid, low = pieces_of(array)
    return jnp.concatenate([high, mid, low, high, mid, high], dim)


def wide_dot(left, right, right_dim=0):
    return bdot(left_pieces(left), right_pieces(right, right_dim), right_dim)


def tile_dot(high_ref, mid_ref, low_ref, right):
    first, second, third = pieces_of(right)
    both = jnp.concatenate([first, second], 1)
    by_high = bdot(high_ref[...], jnp.concatenate([both, third], 1))
    by_mid = bdot(mid_ref[...], both)
    by_low = bdot(low_ref[...], first)
    small = by_high[:, 2 * PAD :] + by_mid[:, PAD:] + by_low
    return by_high[:, :PAD] + (by_high[:, PAD : 2 * PAD] + by_mid[:, :PAD] + small)


def start_copies(sources, targets, sems):
    copies = [pltpu.make_async_copy(s, t, sems.at[n]) for n, (s, t) in enumerate(zip(sources, targets))]
    for copy in copies:
        copy.start()
    return copies


def start_kernel(
    points_hbm, lengths_hbm, probes_hbm, targets_hbm, own_ref, col_ref, points_ref, lengths_ref, probes_ref, targets_ref, sems
):
    refs = (points_ref, lengths_ref, probes_ref, targets_ref)
    for copy in start_copies((points_hbm, lengths_hbm, probes_hbm, targets_hbm), refs, sems):
        copy.wait()
    scaled = points_ref[...] / lengths_ref[...]
    rhs = jnp.concatenate([probes_ref[...], targets_ref[...], jnp.zeros((1, PAD), f32)], 0).T
    pairs = [jnp.concatenate([scaled[16 * g : 16 * g + 8], scaled[16 * g + 8 : 16 * g + 16]], 1) for g in range(2)]
    block = jnp.concatenate(pairs + [pack(rhs)], 0)
    own_ref[...] = block
    col_ref[...] = jnp.broadcast_to(block[None], col_ref.shape)


def norm_lanes(points, first):
    across = lax.broadcasted_iota(jnp.int32, (points.shape[0], 128), 1)
    lanes = jnp.where((across >= 3 - first) & (across < 6 - first), 1.0, 0.0)
    for n, piece in enumerate(pieces_of(jnp.sum(points * points, 1, keepdims=True))):
        lanes = jnp.where(across == first + n, piece.astype(f32), lanes)
    return lanes.astype(bf16)


def tile_kernel(
    row_ref, col_ref, own_ref, slope_hbm, high_hbm, mid_hbm, low_hbm, message_ref, slope_ref, high_ref, mid_ref, low_ref, sems
):
    row_points = unpack_points(row_ref) * root_five
    col_points = unpack_points(col_ref) * root_five
    left = jnp.concatenate([left_pieces(row_points), norm_lanes(row_points, 0)], 1)
    right = jnp.concatenate([right_pieces(-2.0 * col_points, 1), norm_lanes(col_points, 3)], 1)
    slope_ref[...] = bdot(left, right, 1)

    def strip(i, carry):
        here = pl.ds(pl.multiple_of(i * 16, 16), 16)
        squared = jnp.maximum(slope_ref[here, :], 0.0)
        dist = squared * lax.rsqrt(jnp.maximum(squared, 1e-30))
        decayed = jnp.exp(-dist)
        more = 1.0 + dist
        slope_ref[here, :] = more * decayed
        high, mid, low = pieces_of((more + squared * (1.0 / 3.0)) * decayed)
        high_ref[here, :] = high
        mid_ref[here, :] = mid
        low_ref[here, :] = low
        return carry

    lax.fori_loop(0, slope_ref.shape[0] // 16, strip, 0)
    copies = start_copies((slope_ref, high_ref, mid_ref, low_ref), (slope_hbm, high_hbm, mid_hbm, low_hbm), sems)
    row_rhs = unpack_columns(row_ref, 16)
    col_rhs = unpack_columns(col_ref, 16)
    own_rhs = unpack(own_ref[16:24, :])
    partial = tile_dot(high_ref, mid_ref, low_ref, col_rhs)
    curvature = dot(row_rhs, partial, 0, 0)
    gram = dot(own_rhs, own_rhs, 0, 0)
    quarter = partial.shape[0] // 4
    chunks = jnp.concatenate([partial[quarter * g : quarter * g + quarter] for g in range(4)], 1)
    message_ref[:, 0:8, :] = chunks.reshape(quarter // 8, 8, 128)
    grams = pack(join_symmetric(symmetric(curvature), gram))
    message_ref[:, 8:16, :] = jnp.broadcast_to(grams[None], (quarter // 8, 8, 128))
    for copy in copies:
        copy.wait()


def images_kernel(variances_ref, got_ref, own_ref, own_images_ref, row_ref, col_ref):
    summed = jnp.sum(got_ref[...], 0)
    images = variances_ref[0] * summed[0:8] + variances_ref[1] * own_ref[16:24, :]
    own_images_ref[...] = images
    row_ref[...] = jnp.broadcast_to(images[None], row_ref.shape)
    col_ref[...] = jnp.broadcast_to(jnp.concatenate([images, summed[8:16]], 0)[None], col_ref.shape)


def residual_of(rhs, images, advance):
    return rhs - wide_dot(images, advance)


def advance_kernel(
    variances_ref, got_ref, col_ref, high_hbm, mid_hbm, low_hbm, coef_ref, product_ref, high_ref, mid_ref, low_ref, sems
):
    copies = start_copies((high_hbm, mid_hbm, low_hbm), (high_ref, mid_ref, low_ref), sems)
    base_curvature, res_gram = part_symmetric(unpack(jnp.sum(got_ref[:, 8:16, :], 0)))
    curvature = variances_ref[0] * base_curvature + variances_ref[1] * res_gram
    advance, inverse = eliminate(
        [jnp.concatenate([curvature, res_gram], 1), jnp.concatenate([res_gram, identity()], 1)]
    )
    coef_ref[...] = jnp.concatenate([advance, inverse, curvature, jnp.zeros((PAD, PAD), f32)], 1)
    residual = residual_of(unpack_columns(col_ref, 16), unpack_columns(got_ref, 0), advance)
    for copy in copies:
        copy.wait()
    product_ref[...] = tile_dot(high_ref, mid_ref, low_ref, residual)


def grams_kernel(got_ref, row_ref, own_ref, own_images_ref, coef_ref, product_ref, message_ref):
    advance = coef_ref[:, :PAD]
    residual = residual_of(unpack_columns(row_ref, 16), unpack_columns(got_ref, 0), advance)
    own_res = residual_of(unpack(own_ref[16:24, :]), unpack(own_images_ref[...]), advance)
    curvature = dot(residual, product_ref[...], 0, 0)
    gram = dot(own_res, own_res, 0, 0)
    message = pack(join_symmetric(symmetric(curvature), gram))
    message_ref[...] = jnp.broadcast_to(message[None], message_ref.shape)


def spread_kernel(got_ref, out_ref):
    out_ref[...] = jnp.broadcast_to(jnp.sum(got_ref[...], 0)[None], out_ref.shape)


def gradient_kernel(
    total_points,
    variances_ref,
    got_ref,
    coef_ref,
    row_ref,
    col_ref,
    own_ref,
    row_images_ref,
    col_images_ref,
    own_images_ref,
    slope_hbm,
    high_hbm,
    mid_hbm,
    solves_ref,
    terms_ref,
    slope_ref,
    high_ref,
    mid_ref,
    matrix_ref,
    upper_ref,
    lower_ref,
    sums_ref,
    sems,
):
    copies = start_copies((slope_hbm, high_hbm, mid_hbm), (slope_ref, high_ref, mid_ref), sems)
    signal_var, noise_var = variances_ref[0], variances_ref[1]
    advance, inverse, curvature = (coef_ref[:, PAD * g : PAD * g + PAD] for g in range(3))
    base_curvature, next_gram = part_symmetric(unpack(jnp.sum(got_ref[...], 0)))
    carry_over = dot(inverse, next_gram)
    next_curv = (
        signal_var * base_curvature
        + noise_var * next_gram
        - symmetric(dot(carry_over, dot(curvature, carry_over), 0, 0))
    )
    (next_advance,) = eliminate([jnp.concatenate([next_curv, next_gram], 1)])
    rhs_coef = advance + dot(carry_over + identity(), next_advance)
    coef = jnp.concatenate([rhs_coef, -dot(advance, next_advance)], 0)

    def solves_of(rhs, images):
        return wide_dot(jnp.concatenate([rhs, images], 1), coef)

    def pair_of(rhs, solves):
        across = lax.broadcasted_iota(jnp.int32, rhs.shape, 1)
        return jnp.where(across < PROBES, rhs, solves)

    own_rhs = unpack(own_ref[16:24, :])
    own_solves = solves_of(own_rhs, unpack(own_images_ref[...]))
    solves_ref[...] = own_solves.T[0:COLS, :]
    col_rhs = unpack_columns(col_ref, 16)
    col_pair = pair_of(col_rhs, solves_of(col_rhs, unpack_columns(col_images_ref, 0)))
    across = lax.broadcasted_iota(jnp.int32, (1, PAD), 1)
    weights = jnp.where(across < PROBES, -1.0 / PROBES, 1.0) * (0.5 / total_points)
    row_weights = solves_of(unpack_columns(row_ref, 16), unpack_columns(row_images_ref, 0)) * weights
    matrix_ref[...] = wide_dot(row_weights, col_pair, 1)
    for copy in copies:
        copy.wait()

    def strip(i, total):
        here = pl.ds(pl.multiple_of(i * 16, 16), 16)
        values = matrix_ref[here, :]
        weighted = values * slope_ref[here, :]
        upper = weighted.astype(bf16)
        upper_ref[here, :] = upper
        lower_ref[here, :] = (weighted - upper.astype(f32)).astype(bf16)
        sums_ref[here, :] = jnp.broadcast_to(jnp.sum(weighted, 1, keepdims=True), (16, 128))
        return total + values * (high_ref[here, :].astype(f32) + mid_ref[here, :].astype(f32))

    signal = lax.fori_loop(0, matrix_ref.shape[0] // 16, strip, jnp.zeros((16, matrix_ref.shape[1]), f32))
    row_points = unpack_points(row_ref)
    col_points = unpack_points(col_ref)
    right_high, right_low = pieces_of(jnp.concatenate([col_points, col_points * col_points], 1), 2)
    by_upper = bdot(upper_ref[...], jnp.concatenate([right_high, right_low], 1))
    moved = by_upper[:, :128] + (by_upper[:, 128:] + bdot(lower_ref[...], right_high))
    scales = row_points * (row_points * sums_ref[:, :FEAT] - 2.0 * moved[:, :FEAT]) + moved[:, FEAT:128]
    scale_terms = (5.0 / 3.0 * signal_var) * jnp.sum(scales, 0, keepdims=True)
    signal_term = signal_var * jnp.sum(jnp.sum(signal, 0, keepdims=True), 1, keepdims=True)
    noise = jnp.sum(own_solves * weights * pair_of(own_rhs, own_solves), 0, keepdims=True)
    noise_term = noise_var * jnp.sum(noise, 1, keepdims=True)
    terms_ref[...] = jnp.concatenate([scale_terms, signal_term, noise_term, jnp.zeros((1, FEAT - 2), f32)], 1)


def shape_of(*dims, dtype=f32):
    return jax.ShapeDtypeStruct(dims, dtype)


def call(kernel, outs, *operands, scalars=0, far_in=0, far_outs=0, scratch=(), flops=1):
    scalar, near, far = (pl.BlockSpec(memory_space=m) for m in (pltpu.SMEM, pltpu.VMEM, pltpu.HBM))
    near_in = len(operands) - scalars - far_in
    return pl.pallas_call(
        kernel,
        out_shape=outs,
        in_specs=[scalar] * scalars + [near] * near_in + [far] * far_in,
        out_specs=[far] * far_outs + [near] * (len(outs) - far_outs),
        scratch_shapes=scratch,
        compiler_params=PARAMS,
        cost_estimate=pl.CostEstimate(flops=flops, bytes_accessed=1 << 20, transcendentals=0),
    )(*operands)


def exchange(blocks, axis):
    return lax.all_to_all(blocks, axis, 0, 0, tiled=True)


def local(points, length_scales, variances, targets, probe_vectors):
    rows = lax.axis_size("row")
    cols = lax.axis_size("col")
    width = points.shape[1]
    row_block, col_set = cols * width, rows * width
    total_points = width * rows * cols
    tile = (row_block, col_set)
    sems = pltpu.SemaphoreType.DMA((4,))
    values, halves = pltpu.VMEM(tile, f32), pltpu.VMEM(tile, bf16)
    own, to_col = call(
        start_kernel,
        [shape_of(24, 128), shape_of(rows, 24, 128)],
        points.T,
        length_scales[None],
        probe_vectors,
        targets[None],
        far_in=4,
        scratch=[
            pltpu.VMEM((width, FEAT), f32),
            pltpu.VMEM((1, FEAT), f32),
            pltpu.VMEM((PROBES, width), f32),
            pltpu.VMEM((1, width), f32),
            sems,
        ],
    )
    col_got = exchange(to_col, "row")
    row_got = lax.all_gather(own, "col")
    slope, high, mid, low, message = call(
        tile_kernel,
        [shape_of(*tile)] + [shape_of(*tile, dtype=bf16)] * 3 + [shape_of(cols, 16, 128)],
        row_got,
        col_got,
        own,
        far_outs=4,
        scratch=[values, halves, halves, halves, sems],
    )
    own_images, images_row, images_col = call(
        images_kernel,
        [shape_of(8, 128), shape_of(cols, 8, 128), shape_of(rows, 16, 128)],
        variances,
        exchange(message, "col"),
        own,
        scalars=1,
    )
    col_images = exchange(images_col, "row")
    row_images = exchange(images_row, "col")
    coef, product = call(
        advance_kernel,
        [shape_of(PAD, 128), shape_of(row_block, PAD)],
        variances,
        col_images,
        col_got,
        high,
        mid,
        low,
        scalars=1,
        far_in=3,
        scratch=[halves, halves, halves, sems],
    )
    (message,) = call(
        grams_kernel, [shape_of(cols, 8, 128)], row_images, row_got, own, own_images, coef, product
    )
    (message,) = call(spread_kernel, [shape_of(rows, 8, 128)], exchange(message, "col"))
    solves, terms = call(
        functools.partial(gradient_kernel, total_points),
        [shape_of(COLS, width), shape_of(1, 128)],
        variances,
        exchange(message, "row"),
        coef,
        row_got,
        col_got,
        own,
        row_images,
        col_images,
        own_images,
        slope,
        high,
        mid,
        scalars=1,
        far_in=3,
        scratch=[values, halves, halves, values, halves, halves, pltpu.VMEM((row_block, 128), f32), sems],
    )
    terms = jnp.sum(exchange(jnp.broadcast_to(terms[None], (cols, 1, 128)), "col"), 0)
    terms = jnp.sum(exchange(jnp.broadcast_to(terms[None], (rows, 1, 128)), "row"), 0)
    return (solves, terms[0, : FEAT + 2])


def solution(mesh):
    placed = (P(None, ("row", "col")), P(), P(), P(("row", "col")), P(None, ("row", "col")))
    return jax.shard_map(
        local, mesh=mesh, in_specs=placed, out_specs=(P(None, ("row", "col")), P()), check_vma=False
    )
```

time: 181 us -> 160 us (0.88)
  waiting for transfers between devices: 13.2 us -> 0.07 us
  Pallas kernels: 32.7 us -> 25.1 us
  local copies, waits for them, and re-layouts: 14.5 us -> 9.04 us
  blocking collectives: 104 us -> 109 us
    all_gather x0 -> x1, blocking collectives: none -> 24.5 us  [local(): row_got = lax.all_gather(own, 'col')]
    all_to_all x7 -> x6, blocking collectives: 104 us -> 84.2 us  [exchange(): return lax.all_to_all(blocks, axis, 0, 0, tiled=True)]
    all_to_all x2, waiting for transfers between devices: 13.2 us -> 0.07 us  [exchange(): return lax.all_to_all(blocks, axis, 0, 0, tiled=True)]
    pallas_call x6 -> x7, Pallas kernels: 32.7 us -> 25.1 us  [call(): pl.pallas_call(kernel, out_shape=outs, in_specs=[scalar] * scalars + [nea...]
    unnamed x36 -> x20, local copies, waits for them, and re-layouts: 13.3 us -> 8.5 us
where the time goes in v3:
time: 160 us; the launch traced here: 159 us
  blocking collectives  109 us (68%)
  Pallas kernels  25.1 us (16%)
  starting transfers between devices  15.5 us (10%)
  local copies, waits for them, and re-layouts  9.04 us (6%)
    all_to_all x6, blocking collectives, exchange(): return lax.all_to_all(blocks, axis, 0, 0, tiled=True)  84.2 us
    pallas_call x7, Pallas kernels, call(): pl.pallas_call(kernel, out_shape=outs, in_specs=[scalar] * scalars + [nea...  25.1 us
    all_gather x1, blocking collectives, local(): row_got = lax.all_gather(own, 'col')  24.5 us
    all_to_all x2, starting transfers between devices, exchange(): return lax.all_to_all(blocks, axis, 0, 0, tiled=True)  15.5 us
    unnamed x20, local copies, waits for them, and re-layouts  8.5 us
  transfers between devices with their start and end apart: 2, of which 1 were waited for; matrix products, arithmetic and copies ran while one was open for 0% of the time, Pallas kernels for 4%

profile of v3, /device:TPU:1, one launch (start us, length us, event | category | flops | bytes accessed | tf_op | source)
XLA Modules:
  0.0 159.1 jit_solution(6056176099759154259)
XLA Ops:
  0.6 0.0 copy-start.7
  0.6 0.0 copy-start.4
  0.7 0.7 copy-done.4
  1.4 0.0 copy-start.5
  1.4 0.7 copy-done.5
  2.1 0.0 copy-start.8
  2.1 0.7 copy-done.8
  2.7 0.0 copy-start.9
  2.7 0.7 copy-done.9
  3.4 1.0 shard_map.68
  4.4 10.5 %all-to-all-start = ((f32[32,24,128]{2,1,0:T(8,128)}), f32[32,24,128]{2,1,0:T(8,128)S(1)}, u32[]{:S(2)}, u32[]{:S(2)}) async-start(f32[32,24,128]{2,1,0:T(8,128)} %get-tuple-element.17), calls=%async_computation | async-start | bytes 786432 | tf_op jit(solution)/shard_map/all_to_all | solution.py:340
  14.9 24.5 %all-gather = f32[384,128]{1,0:T(8,128)S(1)} all-gather(f32[24,128]{1,0:T(8,128)S(1)} %get-tuple-element.16.own_ref), channel_id=2, replica_groups=mesh['row'=32,'col'=16] {'col'}, dimensions={0}, use_global_device_ids=true | all-gather | bytes 208896 | tf_op jit(solution)/shard_map/all_gather | solution.py:369
  39.4 0.0 all-to-all-done.col_ref
  39.4 5.6 %shard_map.69 = (f32[512,1024]{1,0:T(8,128)S(1)}, bf16[512,1024]{1,0:T(8,128)(2,1)S(1)}, bf16[512,1024]{1,0:T(8,128)(2,1)S(1)}, bf16[512,1024]{1,0:T(8,128)(2,1)S(1)}, f32[16,16,128]{2,1,0:T(8,128)S(1)}) custom-call(f32[16,24,128]{2,1,0:T(8,128)S(1)} %bitcast.10, f32[32,24,128]{2,1,0:T(8,128)S(1)} %all-to-all-done.col_ref, ...), custom_call_target="tpu_custom_call" | custom-call | flops 1 | bytes 1048576 | tf_op jit(solution)/shard_map/pallas_call | solution.py:328
  45.0 0.0 copy-start
  45.0 1.3 copy-done
  46.3 0.0 copy-start.2
  46.3 1.0 copy-done.2
  47.3 11.8 %all_to_all.40.got_ref = f32[16,16,128]{2,1,0:T(8,128)S(1)} all-to-all(f32[16,16,128]{2,1,0:T(8,128)S(1)} %get-tuple-element.18), channel_id=1, replica_groups=mesh['row'=32,'col'=16] {'col'}, dimensions={0} | all-to-all | bytes 262144 | tf_op jit(solution)/shard_map/all_to_all | solution.py:340
  59.1 0.0 copy-start.6
  59.1 0.7 copy-done.6
  59.8 1.2 shard_map.70
  61.0 20.0 %all_to_all.41.got_ref.col_images_ref = f32[32,16,128]{2,1,0:T(8,128)S(1)} all-to-all(f32[32,16,128]{2,1,0:T(8,128)S(1)} %get-tuple-element.21), channel_id=1, replica_groups=mesh['row'=32,'col'=16] {'row'}, dimensions={0} | all-to-all | bytes 524288 | tf_op jit(solution)/shard_map/all_to_all | solution.py:340
  81.0 5.0 %all-to-all-start.2 = ((f32[16,8,128]{2,1,0:T(8,128)}), f32[16,8,128]{2,1,0:T(8,128)S(1)}, u32[]{:S(2)}, u32[]{:S(2)}) async-start(f32[16,8,128]{2,1,0:T(8,128)} %get-tuple-element.19), calls=%async_computation.2 | async-start | bytes 131072 | tf_op jit(solution)/shard_map/all_to_all | solution.py:340
  86.0 0.0 copy-done.7
  86.0 0.0 copy-start.3
  86.0 1.2 copy-done.3
  87.2 6.5 %shard_map.71 = (f32[32,128]{1,0:T(8,128)S(1)}, f32[512,32]{1,0:T(8,128)S(1)}) custom-call(f32[2]{0:T(128)S(1)} %copy-done.7, f32[32,16,128]{2,1,0:T(8,128)S(1)} %all_to_all.41.got_ref.col_images_ref, f32[32,24,128]{2,1,0:T(8,128)S(1)} %all-to-all-done.col_ref, bf16[512,1024]{1,0:T(8,128)(2,1)S(1)} %get-tuple-element.22.high_hbm, ...), custom_call_target="tpu_custom_call" | custom-call | flops 1 | bytes 1048576 | tf_op jit(solution)/shard_map/pallas_call | solution.py:328
  93.7 0.1 all-to-all-done.2.got_ref.row_images_ref
  93.8 0.9 shard_map.72
  94.7 14.8 %all_to_all.42.got_ref = f32[16,8,128]{2,1,0:T(8,128)S(1)} all-to-all(f32[16,8,128]{2,1,0:T(8,128)S(1)} %shard_map.72), channel_id=1, replica_groups=mesh['row'=32,'col'=16] {'col'}, dimensions={0} | all-to-all | bytes 131072 | tf_op jit(solution)/shard_map/all_to_all | solution.py:340
  109.6 14.1 %all_to_all.43.got_ref = f32[32,8,128]{2,1,0:T(8,128)S(1)} all-to-all(f32[32,8,128]{2,1,0:T(8,128)S(1)} %shard_map.73), channel_id=1, replica_groups=mesh['row'=32,'col'=16] {'row'}, dimensions={0} | all-to-all | bytes 262144 | tf_op jit(solution)/shard_map/all_to_all | solution.py:340
  123.6 0.0 copy-start.1
  123.6 1.6 copy-done.1
  125.2 9.9 %shard_map.74 = (f32[31,32]{1,0:T(8,128)}, f32[1,128]{1,0:T(1,128)S(1)}) custom-call(f32[2]{0:T(128)S(1)} %copy-done.7, f32[32,8,128]{2,1,0:T(8,128)S(1)} %all_to_all.43.got_ref, f32[32,128]{1,0:T(8,128)S(1)} %get-tuple-element.25.coef_ref, f32[16,24,128]{2,1,0:T(8,128)S(1)} %bitcast.12, f32[32,24,128]{2,1,0:T(8,128)S(1)} %all-to-all-done.col_ref, ...), custom_call_target="tpu_custom_call" | custom-call | flops 1 | bytes 1048576 | tf_op jit(solution)/shard_map/pallas_call | solution.py:328
  135.1 11.6 %all_to_all.44 = f32[16,1,128]{2,1,0:T(1,128)S(1)} all-to-all(f32[16,1,128]{2,1,0:T(1,128)S(1)} %broadcast_in_dim.23), channel_id=1, replica_groups=mesh['row'=32,'col'=16] {'col'}, dimensions={0} | all-to-all | bytes 16384 | tf_op jit(solution)/shard_map/all_to_all | solution.py:340
  146.7 11.9 %all_to_all.45 = f32[32,1,128]{2,1,0:T(1,128)S(1)} all-to-all(f32[32,1,128]{2,1,0:T(1,128)S(1)} %broadcast_in_dim.24), channel_id=1, replica_groups=mesh['row'=32,'col'=16] {'row'}, dimensions={0} | all-to-all | bytes 32768 | tf_op jit(solution)/shard_map/all_to_all | solution.py:340
  158.6 0.5 slice_bitcast_fusion
  (5 shorter events, 0.1 us)
Async XLA Ops:
  0.6 85.3 %copy-start.7 = (f32[2]{0:T(128)S(1)}, f32[2]{0:T(128)}, u32[]{:S(2)}) copy-start(f32[2]{0:T(128)} %variances_ref.5) | copy-start | bytes 28
  0.6 0.7 copy-start.4
  1.4 0.7 copy-start.5
  2.1 0.7 copy-start.8
  2.7 0.7 copy-start.9
  4.4 35.0 %all-to-all-start = ((f32[32,24,128]{2,1,0:T(8,128)}), f32[32,24,128]{2,1,0:T(8,128)S(1)}, u32[]{:S(2)}, u32[]{:S(2)}) async-start(f32[32,24,128]{2,1,0:T(8,128)} %get-tuple-element.17), calls=%async_computation | async-start | bytes 786432 | tf_op jit(solution)/shard_map/all_to_all | solution.py:340
  45.0 1.3 copy-start
  46.3 1.0 copy-start.2
  59.1 0.7 copy-start.6
  81.0 12.8 %all-to-all-start.2 = ((f32[16,8,128]{2,1,0:T(8,128)}), f32[16,8,128]{2,1,0:T(8,128)S(1)}, u32[]{:S(2)}, u32[]{:S(2)}) async-start(f32[16,8,128]{2,1,0:T(8,128)} %get-tuple-element.19), calls=%async_computation.2 | async-start | bytes 131072 | tf_op jit(solution)/shard_map/all_to_all | solution.py:340
  86.0 1.2 copy-start.3
  123.6 1.6 %copy-start.1 = (f32[512,1024]{1,0:T(8,128)S(1)}, f32[512,1024]{1,0:T(8,128)}, u32[]{:S(2)}) copy-start(f32[512,1024]{1,0:T(8,128)} %copy-done) | copy-start | bytes 6291460

commit v4 on v3

v4 whole, which is shorter than its diff:
```python
import functools

import jax
import jax.numpy as jnp
from jax import lax
from jax.experimental import pallas as pl
from jax.experimental.pallas import tpu as pltpu
from jax.sharding import PartitionSpec as P

PROBES = 30
COLS = 31
FEAT = 64
PAD = 32
PARTS = 4
f32 = jnp.float32
bf16 = jnp.bfloat16
root_five = 5.0**0.5
highest = lax.Precision.HIGHEST
PARAMS = pltpu.CompilerParams(vmem_limit_bytes=60 * 1024 * 1024)


def dot(left, right, left_dim=1, right_dim=0):
    return lax.dot_general(
        left, right, (((left_dim,), (right_dim,)), ((), ())), precision=highest, preferred_element_type=f32
    )


def pack(square):
    return jnp.concatenate([square[8 * g : 8 * g + 8] for g in range(4)], 1)


def unpack(rows):
    return jnp.concatenate([rows[:, PAD * g : PAD * g + PAD] for g in range(4)], 0)


def unpack_columns(ref, start):
    count = ref.shape[0]
    pieces = [ref[:, start : start + 8, PAD * g : PAD * g + PAD].reshape(8 * count, PAD) for g in range(4)]
    return jnp.concatenate(pieces, 0)


def unpack_points(ref):
    count = ref.shape[0]
    pieces = []
    for g in range(4):
        top, left = 8 * (g // 2), FEAT * (g % 2)
        pieces.append(ref[:, top : top + 8, left : left + FEAT].reshape(8 * count, FEAT))
    return jnp.concatenate(pieces, 0)


def places(rows=PAD, columns=PAD):
    shape = (rows, columns)
    return lax.broadcasted_iota(jnp.int32, shape, 0), lax.broadcasted_iota(jnp.int32, shape, 1)


def symmetric(matrix):
    return 0.5 * (matrix + matrix.T)


def join_symmetric(first, second):
    down, across = places()
    diagonal = jnp.sum(jnp.where(down == across, second, 0.0), 0, keepdims=True)
    return jnp.where(down == PAD - 1, diagonal, jnp.where(down >= across, first, second))


def part_symmetric(joined):
    down, across = places()
    inside = down < PAD - 1
    lower = jnp.where((down >= across) & inside, joined, 0.0)
    upper = jnp.where(down < across, joined, 0.0)
    eye = down == across
    first = jnp.where(eye, lower, lower + lower.T)
    second = upper + upper.T + jnp.where(eye, joined[PAD - 1 : PAD, :], 0.0)
    return first, second


def eliminate(systems):
    down, across = places(PAD, 2 * PAD)
    systems = [jnp.where((down == PAD - 1) & (across == PAD - 1), 1.0, system) for system in systems]
    for k in range(0, PAD, 2):
        first, second = down == k, down == k + 1
        for n, system in enumerate(systems):
            top, bottom = system[k : k + 1, :], system[k + 1 : k + 2, :]
            left, right = system[:, k : k + 1], system[:, k + 1 : k + 2]
            one, off, two = left[k : k + 1], right[k : k + 1], right[k + 1 : k + 2]
            scale = 1.0 / (one * two - off * off)
            upper = (two * top - off * bottom) * scale
            lower = (one * bottom - off * top) * scale
            rest = system - left * upper - right * lower
            systems[n] = jnp.where(first, upper, jnp.where(second, lower, rest))
    return [system[:, PAD:] for system in systems]


def identity():
    down, across = places()
    return jnp.where(down == across, 1.0, 0.0)


def pieces_of(array, count=3):
    pieces = []
    for _ in range(count):
        piece = array.astype(bf16)
        pieces.append(piece)
        array = array - piece.astype(f32)
    return pieces


def bdot(left, right, right_dim=0):
    return lax.dot_general(left, right, (((1,), (right_dim,)), ((), ())), preferred_element_type=f32)


def left_pieces(array):
    high, mid, low = pieces_of(array)
    return jnp.concatenate([high, high, high, mid, mid, low], 1)


def right_pieces(array, dim):
    high, mid, low = pieces_of(array)
    return jnp.concatenate([high, mid, low, high, mid, high], dim)


def wide_dot(left, right, right_dim=0):
    return bdot(left_pieces(left), right_pieces(right, right_dim), right_dim)


def tile_dot(tile_ref, right):
    first, second, third = pieces_of(right)
    both = jnp.concatenate([first, second], 1)
    by_high = bdot(tile_ref[0], jnp.concatenate([both, third], 1))
    by_mid = bdot(tile_ref[1], both)
    by_low = bdot(tile_ref[2], first)
    small = by_high[:, 2 * PAD :] + by_mid[:, PAD:] + by_low
    return by_high[:, :PAD] + (by_high[:, PAD : 2 * PAD] + by_mid[:, :PAD] + small)


def start_kernel(joined_ref, own_ref, col_ref):
    scaled = joined_ref[0:32, :FEAT] / joined_ref[63:64, :FEAT]
    down, _ = places()
    rhs = jnp.where(down < COLS, joined_ref[32:64, :PAD], 0.0).T
    pairs = [jnp.concatenate([scaled[16 * g : 16 * g + 8], scaled[16 * g + 8 : 16 * g + 16]], 1) for g in range(2)]
    block = jnp.concatenate(pairs + [pack(rhs)], 0)
    own_ref[...] = block
    col_ref[...] = jnp.broadcast_to(block[None], col_ref.shape)


def variances_of(joined_ref):
    return joined_ref[63:64, FEAT : FEAT + 1], joined_ref[63:64, FEAT + 1 : FEAT + 2]


def norm_lanes(points, first):
    across = lax.broadcasted_iota(jnp.int32, (points.shape[0], 128), 1)
    lanes = jnp.where((across >= 3 - first) & (across < 6 - first), 1.0, 0.0)
    for n, piece in enumerate(pieces_of(jnp.sum(points * points, 1, keepdims=True))):
        lanes = jnp.where(across == first + n, piece.astype(f32), lanes)
    return lanes.astype(bf16)


def tile_kernel(row_ref, col_ref, own_ref, tile_hbm, message_ref, work_ref, tile_ref, sems):
    row_points = unpack_points(row_ref) * root_five
    col_points = unpack_points(col_ref) * root_five
    left = jnp.concatenate([left_pieces(row_points), norm_lanes(row_points, 0)], 1)
    right = jnp.concatenate([right_pieces(-2.0 * col_points, 1), norm_lanes(col_points, 3)], 1)
    work_ref[...] = bdot(left, right, 1)

    def strip(i, carry):
        here = pl.ds(pl.multiple_of(i * 16, 16), 16)
        squared = jnp.maximum(work_ref[here, :], 0.0)
        dist = squared * lax.rsqrt(jnp.maximum(squared, 1e-30))
        decayed = jnp.exp(-dist)
        more = 1.0 + dist
        pieces = pieces_of((more + squared * (1.0 / 3.0)) * decayed) + pieces_of(more * decayed, 2)
        for n, piece in enumerate(pieces):
            tile_ref[n, here, :] = piece
        return carry

    rows = work_ref.shape[0]
    part = rows // PARTS
    copies = []
    for n in range(PARTS):
        lax.fori_loop(n * (part // 16), (n + 1) * (part // 16), strip, 0)
        here = pl.ds(n * part, part)
        copies.append(pltpu.make_async_copy(tile_ref.at[:, here, :], tile_hbm.at[:, here, :], sems.at[n]))
        copies[n].start()
    row_rhs = unpack_columns(row_ref, 16)
    col_rhs = unpack_columns(col_ref, 16)
    own_rhs = unpack(own_ref[16:24, :])
    partial = tile_dot(tile_ref, col_rhs)
    curvature = dot(row_rhs, partial, 0, 0)
    gram = dot(own_rhs, own_rhs, 0, 0)
    quarter = rows // 4
    chunks = jnp.concatenate([partial[quarter * g : quarter * g + quarter] for g in range(4)], 1)
    message_ref[:, 0:8, :] = chunks.reshape(quarter // 8, 8, 128)
    grams = pack(join_symmetric(symmetric(curvature), gram))
    message_ref[:, 8:16, :] = jnp.broadcast_to(grams[None], (quarter // 8, 8, 128))
    for copy in copies:
        copy.wait()


def images_kernel(got_ref, own_ref, joined_ref, own_images_ref, row_ref, col_ref):
    signal_var, noise_var = variances_of(joined_ref)
    summed = jnp.sum(got_ref[...], 0)
    images = signal_var * summed[0:8] + noise_var * own_ref[16:24, :]
    own_images_ref[...] = images
    row_ref[...] = jnp.broadcast_to(images[None], row_ref.shape)
    col_ref[...] = jnp.broadcast_to(jnp.concatenate([images, summed[8:16]], 0)[None], col_ref.shape)


def residual_of(rhs, images, advance):
    return rhs - wide_dot(images, advance)


def advance_kernel(got_ref, col_ref, joined_ref, tile_hbm, coef_ref, product_ref, tile_ref, sems):
    copy = pltpu.make_async_copy(tile_hbm.at[0:3], tile_ref, sems.at[0])
    copy.start()
    signal_var, noise_var = variances_of(joined_ref)
    base_curvature, res_gram = part_symmetric(unpack(jnp.sum(got_ref[:, 8:16, :], 0)))
    curvature = signal_var * base_curvature + noise_var * res_gram
    advance, inverse = eliminate(
        [jnp.concatenate([curvature, res_gram], 1), jnp.concatenate([res_gram, identity()], 1)]
    )
    residual = residual_of(unpack_columns(col_ref, 16), unpack_columns(got_ref, 0), advance)
    copy.wait()
    product_ref[...] = tile_dot(tile_ref, residual)
    middle = dot(inverse, dot(curvature, inverse))
    coef_ref[...] = jnp.concatenate([advance, inverse, symmetric(middle), jnp.zeros((PAD, PAD), f32)], 1)


def grams_kernel(got_ref, row_ref, own_ref, own_images_ref, coef_ref, product_ref, message_ref):
    advance = coef_ref[:, :PAD]
    residual = residual_of(unpack_columns(row_ref, 16), unpack_columns(got_ref, 0), advance)
    own_res = residual_of(unpack(own_ref[16:24, :]), unpack(own_images_ref[...]), advance)
    curvature = dot(residual, product_ref[...], 0, 0)
    gram = dot(own_res, own_res, 0, 0)
    message = pack(join_symmetric(symmetric(curvature), gram))
    message_ref[...] = jnp.broadcast_to(message[None], message_ref.shape)


def prepare_kernel(row_ref, col_ref, row_images_ref, col_images_ref, left_ref, right_ref, points_ref, moments_ref):
    left_ref[...] = left_pieces(jnp.concatenate([unpack_columns(row_ref, 16), unpack_columns(row_images_ref, 0)], 1))
    right = jnp.concatenate([unpack_columns(col_ref, 16), unpack_columns(col_images_ref, 0)], 1)
    right_ref[...] = right_pieces(right, 1)
    points_ref[...] = unpack_points(row_ref)
    col_points = unpack_points(col_ref)
    moments = pieces_of(jnp.concatenate([col_points, col_points * col_points], 1), 2)
    moments_ref[...] = jnp.concatenate(moments, 1)


def spread_kernel(got_ref, out_ref):
    out_ref[...] = jnp.broadcast_to(jnp.sum(got_ref[...], 0)[None], out_ref.shape)


def gradient_kernel(
    total_points,
    got_ref,
    coef_ref,
    own_ref,
    own_images_ref,
    joined_ref,
    left_ref,
    right_ref,
    points_ref,
    moments_ref,
    tile_hbm,
    solves_ref,
    terms_ref,
    tile_ref,
    matrix_ref,
    weighted_ref,
    sums_ref,
    sems,
):
    copies = []
    for n, k in enumerate((0, 1, 3, 4)):
        copies.append(pltpu.make_async_copy(tile_hbm.at[k], tile_ref.at[n], sems.at[n]))
        copies[n].start()
    signal_var, noise_var = variances_of(joined_ref)
    advance, inverse, middle = (coef_ref[:, PAD * g : PAD * g + PAD] for g in range(3))
    base_curvature, next_gram = part_symmetric(unpack(jnp.sum(got_ref[...], 0)))
    next_curv = signal_var * base_curvature + noise_var * next_gram - symmetric(dot(dot(next_gram, middle), next_gram))
    carry_over = dot(inverse, next_gram)
    (next_advance,) = eliminate([jnp.concatenate([next_curv, next_gram], 1)])
    coef = wide_dot(jnp.concatenate([identity() + carry_over, -advance], 0), next_advance)
    coef = coef + jnp.concatenate([advance, jnp.zeros((PAD, PAD), f32)], 0)
    _, across = places(2 * PAD, PAD)
    weights = jnp.where(across < PROBES, -1.0 / PROBES, 1.0) * (0.5 / total_points)
    target = jnp.where(across == PROBES, coef, 0.0)
    form = dot(target * (0.5 / total_points), target, 1, 1)
    probes = jnp.where(across < PROBES, coef * weights, 0.0)
    form = form + jnp.concatenate([probes, jnp.zeros((2 * PAD, PAD), f32)], 1)
    left = bdot(left_ref[...], right_pieces(form, 0))
    matrix_ref[...] = bdot(left_pieces(left), right_ref[...], 1)

    own_rhs = unpack(own_ref[16:24, :])
    own_solves = dot(jnp.concatenate([own_rhs, unpack(own_images_ref[...])], 1), coef)
    solves_ref[...] = own_solves.T[0:COLS, :]
    pair = jnp.where(across[:PAD] < PROBES, own_rhs, own_solves)
    noise = jnp.sum(own_solves * weights[:PAD] * pair, 0, keepdims=True)
    noise_term = noise_var * jnp.sum(noise, 1, keepdims=True)
    for copy in copies:
        copy.wait()

    def strip(i, total):
        here = pl.ds(pl.multiple_of(i * 16, 16), 16)
        values = matrix_ref[here, :]
        high, mid, slope_high, slope_low = (tile_ref[n, here, :].astype(f32) for n in range(4))
        weighted = values * (slope_high + slope_low)
        upper = weighted.astype(bf16)
        weighted_ref[0, here, :] = upper
        weighted_ref[1, here, :] = (weighted - upper.astype(f32)).astype(bf16)
        sums_ref[here, :] = jnp.broadcast_to(jnp.sum(weighted, 1, keepdims=True), (16, 128))
        return total + values * (high + mid)

    signal = lax.fori_loop(0, matrix_ref.shape[0] // 16, strip, jnp.zeros((16, matrix_ref.shape[1]), f32))
    by_upper = bdot(weighted_ref[0], moments_ref[...])
    moved = by_upper[:, :128] + (by_upper[:, 128:] + bdot(weighted_ref[1], moments_ref[:, :128]))
    points = points_ref[...]
    scales = points * (points * sums_ref[:, :FEAT] - 2.0 * moved[:, :FEAT]) + moved[:, FEAT:128]
    scale_terms = (5.0 / 3.0 * signal_var) * jnp.sum(scales, 0, keepdims=True)
    signal_term = signal_var * jnp.sum(jnp.sum(signal, 0, keepdims=True), 1, keepdims=True)
    terms_ref[...] = jnp.concatenate([scale_terms, signal_term, noise_term, jnp.zeros((1, FEAT - 2), f32)], 1)


def shape_of(*dims, dtype=f32):
    return jax.ShapeDtypeStruct(dims, dtype)


def call(kernel, outs, *operands, far_in=0, far_outs=0, scratch=(), flops=1):
    near, far = (pl.BlockSpec(memory_space=m) for m in (pltpu.VMEM, pltpu.HBM))
    return pl.pallas_call(
        kernel,
        out_shape=outs,
        in_specs=[near] * (len(operands) - far_in) + [far] * far_in,
        out_specs=[far] * far_outs + [near] * (len(outs) - far_outs),
        scratch_shapes=scratch,
        compiler_params=PARAMS,
        cost_estimate=pl.CostEstimate(flops=flops, bytes_accessed=1 << 20, transcendentals=0),
    )(*operands)


def exchange(blocks, axis):
    return lax.all_to_all(blocks, axis, 0, 0, tiled=True)


def local(points, length_scales, variances, targets, probe_vectors):
    rows = lax.axis_size("row")
    cols = lax.axis_size("col")
    width = points.shape[1]
    row_block, col_set = cols * width, rows * width
    total_points = width * rows * cols
    tile = (row_block, col_set)
    sems = pltpu.SemaphoreType.DMA((4,))

    def widen(array):
        return jnp.pad(array, ((0, 0), (0, 128 - array.shape[1])))

    scalars = jnp.concatenate([length_scales, variances])
    joined = jnp.concatenate([widen(a) for a in (points.T, probe_vectors, targets[None], scalars[None])], 0)
    own, to_col = call(start_kernel, [shape_of(24, 128), shape_of(rows, 24, 128)], joined)
    col_got = exchange(to_col, "row")
    row_got = lax.all_gather(own, "col")
    stack, message = call(
        tile_kernel,
        [shape_of(5, *tile, dtype=bf16), shape_of(cols, 16, 128)],
        row_got,
        col_got,
        own,
        far_outs=1,
        scratch=[pltpu.VMEM(tile, f32), pltpu.VMEM((5,) + tile, bf16), sems],
    )
    own_images, images_row, images_col = call(
        images_kernel,
        [shape_of(8, 128), shape_of(cols, 8, 128), shape_of(rows, 16, 128)],
        exchange(message, "col"),
        own,
        joined,
    )
    col_images = exchange(images_col, "row")
    row_images = exchange(images_row, "col")
    coef, product = call(
        advance_kernel,
        [shape_of(PAD, 128), shape_of(row_block, PAD)],
        col_images,
        col_got,
        joined,
        stack,
        far_in=1,
        scratch=[pltpu.VMEM((3,) + tile, bf16), sems],
    )
    (message,) = call(
        grams_kernel, [shape_of(cols, 8, 128)], row_images, row_got, own, own_images, coef, product
    )
    prepared = call(
        prepare_kernel,
        [
            shape_of(row_block, 12 * PAD, dtype=bf16),
            shape_of(col_set, 12 * PAD, dtype=bf16),
            shape_of(row_block, FEAT),
            shape_of(col_set, 4 * FEAT, dtype=bf16),
        ],
        row_got,
        col_got,
        row_images,
        col_images,
    )
    (message,) = call(spread_kernel, [shape_of(rows, 8, 128)], exchange(message, "col"))
    solves, terms = call(
        functools.partial(gradient_kernel, total_points),
        [shape_of(COLS, width), shape_of(1, 128)],
        exchange(message, "row"),
        coef,
        own,
        own_images,
        joined,
        *prepared,
        stack,
        far_in=1,
        scratch=[
            pltpu.VMEM((4,) + tile, bf16),
            pltpu.VMEM(tile, f32),
            pltpu.VMEM((2,) + tile, bf16),
            pltpu.VMEM((row_block, 128), f32),
            sems,
        ],
    )
    terms = jnp.sum(exchange(jnp.broadcast_to(terms[None], (cols, 1, 128)), "col"), 0)
    terms = jnp.sum(exchange(jnp.broadcast_to(terms[None], (rows, 1, 128)), "row"), 0)
    return (solves, terms[0, : FEAT + 2])


def solution(mesh):
    placed = (P(None, ("row", "col")), P(), P(), P(("row", "col")), P(None, ("row", "col")))
    return jax.shard_map(
        local, mesh=mesh, in_specs=placed, out_specs=(P(None, ("row", "col")), P()), check_vma=False
    )
```

time: 160 us -> 168 us (1.050)
  Pallas kernels: 25.1 us -> 36.2 us
  blocking collectives: 109 us -> 98.4 us
  waiting for transfers between devices: 0.07 us -> 6.04 us
  local copies, waits for them, and re-layouts: 9.04 us -> 3.22 us
  starting transfers between devices: 15.5 us -> 20.6 us
  other arithmetic: 0.04 us -> 2.16 us
    all_to_all x6 -> x5, blocking collectives: 84.2 us -> 72.3 us  [exchange(): return lax.all_to_all(blocks, axis, 0, 0, tiled=True)]
    pallas_call x7 -> x8, Pallas kernels: 25.1 us -> 36.2 us  [call(): pl.pallas_call(kernel, out_shape=outs, in_specs=[near] * (len(operands) -...]
    unnamed x20 -> x6, local copies, waits for them, and re-layouts: 8.5 us -> 2.03 us
    all_to_all x2 -> x3, waiting for transfers between devices: 0.07 us -> 6.04 us  [exchange(): return lax.all_to_all(blocks, axis, 0, 0, tiled=True)]
    all_to_all x2 -> x3, starting transfers between devices: 15.5 us -> 20.6 us  [exchange(): return lax.all_to_all(blocks, axis, 0, 0, tiled=True)]
  transfers between devices with their start and end apart: 2 -> 3, of which waited for: 1 -> 2; matrix products, arithmetic and copies ran while one was open for 0% -> 0% of each run, Pallas kernels for 4% -> 7%
where the time goes in v4:
time: 168 us; the launch traced here: 167 us
  blocking collectives  98.4 us (59%)
  Pallas kernels  36.2 us (22%)
  starting transfers between devices  20.6 us (12%)
  waiting for transfers between devices  6.04 us (4%)
  local copies, waits for them, and re-layouts  3.22 us (2%)
  other arithmetic  2.16 us (1%)
    all_to_all x5, blocking collectives, exchange(): return lax.all_to_all(blocks, axis, 0, 0, tiled=True)  72.3 us
    pallas_call x8, Pallas kernels, call(): pl.pallas_call(kernel, out_shape=outs, in_specs=[near] * (len(operands) -...  36.2 us
    all_gather x1, blocking collectives, local(): row_got = lax.all_gather(own, 'col')  26.1 us
    all_to_all x3, starting transfers between devices, exchange(): return lax.all_to_all(blocks, axis, 0, 0, tiled=True)  20.6 us
    all_to_all x3, waiting for transfers between devices, exchange(): return lax.all_to_all(blocks, axis, 0, 0, tiled=True)  6.04 us
  transfers between devices with their start and end apart: 3, of which 2 were waited for; matrix products, arithmetic and copies ran while one was open for 0% of the time, Pallas kernels for 7%

profile of v4, /device:TPU:1, one launch (start us, length us, event | category | flops | bytes accessed | tf_op | source)
XLA Modules:
  0.0 167.3 jit_solution(7816509012764897483)
XLA Ops:
  0.6 0.7 maximum_bitcast_fusion
  1.4 1.4 select_maximum_fusion.joined_ref
  2.8 1.7 shard_map.68
  4.4 10.5 %all-to-all-start = ((f32[32,24,128]{2,1,0:T(8,128)}), f32[32,24,128]{2,1,0:T(8,128)S(1)}, u32[]{:S(2)}, u32[]{:S(2)}) async-start(f32[32,24,128]{2,1,0:T(8,128)} %get-tuple-element.18), calls=%async_computation | async-start | bytes 786432 | tf_op jit(solution)/shard_map/all_to_all | solution.py:341
  14.9 26.1 %all-gather = f32[384,128]{1,0:T(8,128)} all-gather(f32[24,128]{1,0:T(8,128)} %get-tuple-element.17.own_ref), channel_id=2, replica_groups=mesh['row'=32,'col'=16] {'col'}, dimensions={0}, use_global_device_ids=true | all-gather | bytes 208896 | tf_op jit(solution)/shard_map/all_gather | solution.py:360
  41.0 0.0 all-to-all-done.col_ref
  41.0 0.0 copy-start
  41.0 0.8 copy-done
  41.8 7.1 %shard_map.69 = (bf16[5,512,1024]{2,1,0:T(8,128)(2,1)}, f32[16,16,128]{2,1,0:T(8,128)}) custom-call(f32[16,24,128]{2,1,0:T(8,128)} %bitcast.11, f32[32,24,128]{2,1,0:T(8,128)} %copy-done, f32[24,128]{1,0:T(8,128)} %get-tuple-element.17.own_ref), custom_call_target="tpu_custom_call" | custom-call | flops 1 | bytes 1048576 | tf_op jit(solution)/shard_map/pallas_call | solution.py:329
  48.9 13.4 %all_to_all.40.got_ref = f32[16,16,128]{2,1,0:T(8,128)} all-to-all(f32[16,16,128]{2,1,0:T(8,128)} %get-tuple-element.19), channel_id=1, replica_groups=mesh['row'=32,'col'=16] {'col'}, dimensions={0} | all-to-all | bytes 262144 | tf_op jit(solution)/shard_map/all_to_all | solution.py:341
  62.2 1.8 %shard_map.70 = (f32[8,128]{1,0:T(8,128)}, f32[16,8,128]{2,1,0:T(8,128)}, f32[32,16,128]{2,1,0:T(8,128)}) custom-call(f32[16,16,128]{2,1,0:T(8,128)} %all_to_all.40.got_ref, f32[24,128]{1,0:T(8,128)} %get-tuple-element.17.own_ref, f32[64,128]{1,0:T(8,128)} %select_maximum_fusion.joined_ref), custom_call_target="tpu_custom_call" | custom-call | flops 1 | bytes 1048576 | tf_op jit(solution)/shard_map/pallas_call | solution.py:329
  64.0 20.3 %all_to_all.41.got_ref.col_images_ref = f32[32,16,128]{2,1,0:T(8,128)} all-to-all(f32[32,16,128]{2,1,0:T(8,128)} %get-tuple-element.22), channel_id=1, replica_groups=mesh['row'=32,'col'=16] {'row'}, dimensions={0} | all-to-all | bytes 524288 | tf_op jit(solution)/shard_map/all_to_all | solution.py:341
  84.4 5.0 %all-to-all-start.2 = ((f32[16,8,128]{2,1,0:T(8,128)}), f32[16,8,128]{2,1,0:T(8,128)S(1)}, u32[]{:S(2)}, u32[]{:S(2)}) async-start(f32[16,8,128]{2,1,0:T(8,128)} %get-tuple-element.20), calls=%async_computation.2 | async-start | bytes 131072 | tf_op jit(solution)/shard_map/all_to_all | solution.py:341
  89.3 7.8 %shard_map.71 = (f32[32,128]{1,0:T(8,128)}, f32[512,32]{1,0:T(8,128)}) custom-call(f32[32,16,128]{2,1,0:T(8,128)} %all_to_all.41.got_ref.col_images_ref, f32[32,24,128]{2,1,0:T(8,128)} %copy-done, f32[64,128]{1,0:T(8,128)} %select_maximum_fusion.joined_ref, bf16[5,512,1024]{2,1,0:T(8,128)(2,1)} %get-tuple-element.23.tile_hbm), custom_call_target="tpu_custom_call" | custom-call | flops 1 | bytes 1048576 | tf_op jit(solution)/shard_map/pallas_call | solution.py:329
  97.1 0.1 all-to-all-done.2.got_ref.row_images_ref
  97.2 0.0 copy-start.1
  97.2 0.6 copy-done.1
  97.8 2.7 %shard_map.72 = f32[16,8,128]{2,1,0:T(8,128)} custom-call(f32[16,8,128]{2,1,0:T(8,128)} %copy-done.1, f32[16,24,128]{2,1,0:T(8,128)} %bitcast.12, f32[24,128]{1,0:T(8,128)} %get-tuple-element.17.own_ref, f32[8,128]{1,0:T(8,128)} %get-tuple-element.21.own_images_ref, f32[32,128]{1,0:T(8,128)} %get-tuple-element.24.coef_ref, ...), custom_call_target="tpu_custom_call" | custom-call | flops 1 | bytes 1048576 | tf_op jit(solution)/shard_map/pallas_call | solution.py:329
  100.5 15.1 %all_to_all.42.got_ref = f32[16,8,128]{2,1,0:T(8,128)} all-to-all(f32[16,8,128]{2,1,0:T(8,128)} %shard_map.72), channel_id=1, replica_groups=mesh['row'=32,'col'=16] {'col'}, dimensions={0} | all-to-all | bytes 131072 | tf_op jit(solution)/shard_map/all_to_all | solution.py:341
  115.6 1.5 shard_map.73
  117.1 5.1 %all-to-all-start.5 = ((f32[32,8,128]{2,1,0:T(8,128)}), f32[32,8,128]{2,1,0:T(8,128)S(1)}, u32[]{:S(2)}, u32[]{:S(2)}) async-start(f32[32,8,128]{2,1,0:T(8,128)} %shard_map.73), calls=%async_computation.5 | async-start | bytes 262144 | tf_op jit(solution)/shard_map/all_to_all | solution.py:341
  122.2 3.2 %shard_map.74 = (bf16[512,384]{1,0:T(8,128)(2,1)}, bf16[1024,384]{1,0:T(8,128)(2,1)}, f32[512,64]{1,0:T(8,128)}, bf16[1024,256]{1,0:T(8,128)(2,1)}) custom-call(f32[16,24,128]{2,1,0:T(8,128)} %bitcast.13, f32[32,24,128]{2,1,0:T(8,128)} %copy-done, f32[16,8,128]{2,1,0:T(8,128)} %copy-done.1, f32[32,16,128]{2,1,0:T(8,128)} %all_to_all.41.got_ref.col_images_ref), custom_call_target="tpu_custom_call" | custom-call | flops 1 | bytes 1048576 | tf_op jit(solution)/shard_map/pallas_call | solution.py:329
  125.4 6.0 %all-to-all-done.5.got_ref = f32[32,8,128]{2,1,0:T(8,128)S(1)} async-done(((f32[32,8,128]{2,1,0:T(8,128)}), f32[32,8,128]{2,1,0:T(8,128)S(1)}, u32[]{:S(2)}, u32[]{:S(2)}) %all-to-all-start.5) | async-done | bytes 131104 | tf_op jit(solution)/shard_map/all_to_all | solution.py:341
  131.4 0.0 copy-start.2
  131.4 0.6 copy-done.2
  132.0 10.6 %shard_map.75 = (f32[31,32]{1,0:T(8,128)}, f32[1,128]{1,0:T(1,128)}) custom-call(f32[32,8,128]{2,1,0:T(8,128)} %copy-done.2, f32[32,128]{1,0:T(8,128)} %get-tuple-element.24.coef_ref, f32[24,128]{1,0:T(8,128)} %get-tuple-element.17.own_ref, f32[8,128]{1,0:T(8,128)} %get-tuple-element.21.own_images_ref, f32[64,128]{1,0:T(8,128)} %select_maximum_fusion.joined_ref, ...), custom_call_target="tpu_custom_call" | custom-call | flops 1 | bytes 1048576 | tf_op jit(solution)/shard_map/pallas_call | solution.py:329
  142.6 0.7 broadcast_in_dim.23
  143.3 11.5 %all_to_all.43 = f32[16,1,128]{2,1,0:T(1,128)S(1)} all-to-all(f32[16,1,128]{2,1,0:T(1,128)S(1)} %broadcast_in_dim.23), channel_id=1, replica_groups=mesh['row'=32,'col'=16] {'col'}, dimensions={0} | all-to-all | bytes 16384 | tf_op jit(solution)/shard_map/all_to_all | solution.py:341
  154.8 11.9 %all_to_all.44 = f32[32,1,128]{2,1,0:T(1,128)S(1)} all-to-all(f32[32,1,128]{2,1,0:T(1,128)S(1)} %broadcast_in_dim.24), channel_id=1, replica_groups=mesh['row'=32,'col'=16] {'row'}, dimensions={0} | all-to-all | bytes 32768 | tf_op jit(solution)/shard_map/all_to_all | solution.py:341
  166.8 0.5 slice_bitcast_fusion
  (3 shorter events, 0.1 us)
Async XLA Ops:
  4.4 36.6 %all-to-all-start = ((f32[32,24,128]{2,1,0:T(8,128)}), f32[32,24,128]{2,1,0:T(8,128)S(1)}, u32[]{:S(2)}, u32[]{:S(2)}) async-start(f32[32,24,128]{2,1,0:T(8,128)} %get-tuple-element.18), calls=%async_computation | async-start | bytes 786432 | tf_op jit(solution)/shard_map/all_to_all | solution.py:341
  41.0 0.8 copy-start
  84.4 12.8 %all-to-all-start.2 = ((f32[16,8,128]{2,1,0:T(8,128)}), f32[16,8,128]{2,1,0:T(8,128)S(1)}, u32[]{:S(2)}, u32[]{:S(2)}) async-start(f32[16,8,128]{2,1,0:T(8,128)} %get-tuple-element.20), calls=%async_computation.2 | async-start | bytes 131072 | tf_op jit(solution)/shard_map/all_to_all | solution.py:341
  97.2 0.6 copy-start.1
  117.1 14.3 %all-to-all-start.5 = ((f32[32,8,128]{2,1,0:T(8,128)}), f32[32,8,128]{2,1,0:T(8,128)S(1)}, u32[]{:S(2)}, u32[]{:S(2)}) async-start(f32[32,8,128]{2,1,0:T(8,128)} %shard_map.73), calls=%async_computation.5 | async-start | bytes 262144 | tf_op jit(solution)/shard_map/all_to_all | solution.py:341
  131.4 0.6 copy-start.2

commit v5 on v4

--- a/solution.py
+++ b/solution.py
@@ -16,7 +16,7 @@
 bf16 = jnp.bfloat16
 root_five = 5.0**0.5
 highest = lax.Precision.HIGHEST
-PARAMS = pltpu.CompilerParams(vmem_limit_bytes=60 * 1024 * 1024)
+NEAR, LARGE = 16 * 1024 * 1024, 50 * 1024 * 1024
 
 
 def dot(left, right, left_dim=1, right_dim=0):
@@ -144,7 +144,7 @@
 
 
 def variances_of(joined_ref):
-    return joined_ref[63:64, FEAT : FEAT + 1], joined_ref[63:64, FEAT + 1 : FEAT + 2]
+    return joined_ref[64:65, 0:1], joined_ref[64:65, 1:2]
 
 
 def norm_lanes(points, first):
@@ -324,7 +324,7 @@
     return jax.ShapeDtypeStruct(dims, dtype)
 
 
-def call(kernel, outs, *operands, far_in=0, far_outs=0, scratch=(), flops=1):
+def call(kernel, outs, *operands, far_in=0, far_outs=0, scratch=(), limit=NEAR):
     near, far = (pl.BlockSpec(memory_space=m) for m in (pltpu.VMEM, pltpu.HBM))
     return pl.pallas_call(
         kernel,
@@ -332,8 +332,8 @@
         in_specs=[near] * (len(operands) - far_in) + [far] * far_in,
         out_specs=[far] * far_outs + [near] * (len(outs) - far_outs),
         scratch_shapes=scratch,
-        compiler_params=PARAMS,
-        cost_estimate=pl.CostEstimate(flops=flops, bytes_accessed=1 << 20, transcendentals=0),
+        compiler_params=pltpu.CompilerParams(vmem_limit_bytes=limit),
+        cost_estimate=pl.CostEstimate(flops=1, bytes_accessed=1 << 20, transcendentals=0),
     )(*operands)
 
 
@@ -353,8 +353,8 @@
     def widen(array):
         return jnp.pad(array, ((0, 0), (0, 128 - array.shape[1])))
 
-    scalars = jnp.concatenate([length_scales, variances])
-    joined = jnp.concatenate([widen(a) for a in (points.T, probe_vectors, targets[None], scalars[None])], 0)
+    parts = (points.T, probe_vectors, targets[None], length_scales[None], variances[None])
+    joined = jnp.concatenate([widen(a) for a in parts], 0)
     own, to_col = call(start_kernel, [shape_of(24, 128), shape_of(rows, 24, 128)], joined)
     col_got = exchange(to_col, "row")
     row_got = lax.all_gather(own, "col")
@@ -365,6 +365,7 @@
         col_got,
         own,
         far_outs=1,
+        limit=LARGE,
         scratch=[pltpu.VMEM(tile, f32), pltpu.VMEM((5,) + tile, bf16), sems],
     )
     own_images, images_row, images_col = call(
@@ -384,6 +385,7 @@
         joined,
         stack,
         far_in=1,
+        limit=LARGE,
         scratch=[pltpu.VMEM((3,) + tile, bf16), sems],
     )
     (message,) = call(
@@ -414,6 +416,7 @@
         *prepared,
         stack,
         far_in=1,
+        limit=LARGE,
         scratch=[
             pltpu.VMEM((4,) + tile, bf16),
             pltpu.VMEM(tile, f32),

time: 168 us -> 156 us (0.929)
  Pallas kernels: 36.2 us -> 27.5 us
  blocking collectives: 98.4 us -> 94.5 us
  waiting for transfers between devices: 6.04 us -> 8.19 us
  other arithmetic: 2.16 us -> 0.04 us
    pallas_call x8, Pallas kernels: 36.2 us -> 27.5 us  [call(): pl.pallas_call(kernel, out_shape=outs, in_specs=[near] * (len(operands) -...]
    pad x0 -> x5, local copies, waits for them, and re-layouts: none -> 3.42 us  [widen(): return jnp.pad(array, ((0, 0), (0, 128 - array.shape[1])))]
    all_to_all x5, blocking collectives: 72.3 us -> 70.1 us  [exchange(): return lax.all_to_all(blocks, axis, 0, 0, tiled=True)]
    all_to_all x3, waiting for transfers between devices: 6.04 us -> 8.19 us  [exchange(): return lax.all_to_all(blocks, axis, 0, 0, tiled=True)]
    unnamed x6 -> x0, local copies, waits for them, and re-layouts: 2.03 us -> none
  transfers between devices with their start and end apart: 3 -> 3, of which waited for: 2 -> 2; matrix products, arithmetic and copies ran while one was open for 0% -> 0% of each run, Pallas kernels for 7% -> 6%
where the time goes in v5:
time: 156 us
  blocking collectives  94.5 us (61%)
  Pallas kernels  27.5 us (18%)
  starting transfers between devices  20.6 us (13%)
  waiting for transfers between devices  8.19 us (5%)
  local copies, waits for them, and re-layouts  4 us (3%)
    all_to_all x5, blocking collectives, exchange(): return lax.all_to_all(blocks, axis, 0, 0, tiled=True)  70.1 us
    pallas_call x8, Pallas kernels, call(): pl.pallas_call(kernel, out_shape=outs, in_specs=[near] * (len(operands) -...  27.5 us
    all_gather x1, blocking collectives, local(): row_got = lax.all_gather(own, 'col')  24.5 us
    all_to_all x3, starting transfers between devices, exchange(): return lax.all_to_all(blocks, axis, 0, 0, tiled=True)  20.6 us
    all_to_all x3, waiting for transfers between devices, exchange(): return lax.all_to_all(blocks, axis, 0, 0, tiled=True)  8.19 us
    pad x5, local copies, waits for them, and re-layouts, widen(): return jnp.pad(array, ((0, 0), (0, 128 - array.shape[1])))  3.42 us
  transfers between devices with their start and end apart: 3, of which 2 were waited for; matrix products, arithmetic and copies ran while one was open for 0% of the time, Pallas kernels for 6%

profile of v5, /device:TPU:1, one launch (start us, length us, event | category | flops | bytes accessed | tf_op | source)
XLA Modules:
  0.0 155.6 jit_solution(2629909862855747810)
XLA Ops:
  0.6 0.7 pad.23
  1.3 0.7 pad.24
  2.0 0.7 pad.22
  2.6 0.7 pad.20
  3.3 0.7 pad.21
  4.1 0.9 shard_map.68
  5.0 10.5 %all-to-all-start = ((f32[32,24,128]{2,1,0:T(8,128)}), f32[32,24,128]{2,1,0:T(8,128)S(1)}, u32[]{:S(2)}, u32[]{:S(2)}) async-start(f32[32,24,128]{2,1,0:T(8,128)} %get-tuple-element.18), calls=%async_computation | async-start | bytes 786432 | tf_op jit(solution)/shard_map/all_to_all | solution.py:341
  15.5 24.5 %all-gather = f32[384,128]{1,0:T(8,128)S(1)} all-gather(f32[24,128]{1,0:T(8,128)S(1)} %get-tuple-element.17.own_ref), channel_id=2, replica_groups=mesh['row'=32,'col'=16] {'col'}, dimensions={0}, use_global_device_ids=true | all-gather | bytes 208896 | tf_op jit(solution)/shard_map/all_gather | solution.py:360
  40.0 0.0 all-to-all-done.col_ref
  40.0 5.4 %shard_map.69 = (bf16[5,512,1024]{2,1,0:T(8,128)(2,1)}, f32[16,16,128]{2,1,0:T(8,128)S(1)}) custom-call(f32[16,24,128]{2,1,0:T(8,128)S(1)} %bitcast.11, f32[32,24,128]{2,1,0:T(8,128)S(1)} %all-to-all-done.col_ref, f32[24,128]{1,0:T(8,128)S(1)} %get-tuple-element.17.own_ref), custom_call_target="tpu_custom_call" | custom-call | flops 1 | bytes 1048576 | tf_op jit(solution)/shard_map/pallas_call | solution.py:329
  45.4 11.9 %all_to_all.40.got_ref = f32[16,16,128]{2,1,0:T(8,128)S(1)} all-to-all(f32[16,16,128]{2,1,0:T(8,128)S(1)} %get-tuple-element.19), channel_id=1, replica_groups=mesh['row'=32,'col'=16] {'col'}, dimensions={0} | all-to-all | bytes 262144 | tf_op jit(solution)/shard_map/all_to_all | solution.py:341
  57.3 0.7 shard_map.70
  58.0 20.0 %all_to_all.41.got_ref.col_images_ref = f32[32,16,128]{2,1,0:T(8,128)S(1)} all-to-all(f32[32,16,128]{2,1,0:T(8,128)S(1)} %get-tuple-element.22), channel_id=1, replica_groups=mesh['row'=32,'col'=16] {'row'}, dimensions={0} | all-to-all | bytes 524288 | tf_op jit(solution)/shard_map/all_to_all | solution.py:341
  78.0 5.0 %all-to-all-start.2 = ((f32[16,8,128]{2,1,0:T(8,128)}), f32[16,8,128]{2,1,0:T(8,128)S(1)}, u32[]{:S(2)}, u32[]{:S(2)}) async-start(f32[16,8,128]{2,1,0:T(8,128)} %get-tuple-element.20), calls=%async_computation.2 | async-start | bytes 131072 | tf_op jit(solution)/shard_map/all_to_all | solution.py:341
  83.0 7.7 %shard_map.71 = (f32[32,128]{1,0:T(8,128)S(1)}, f32[512,32]{1,0:T(8,128)S(1)}) custom-call(f32[32,16,128]{2,1,0:T(8,128)S(1)} %all_to_all.41.got_ref.col_images_ref, f32[32,24,128]{2,1,0:T(8,128)S(1)} %all-to-all-done.col_ref, f32[65,128]{1,0:T(8,128)S(1)} %concatenate.3.joined_ref, bf16[5,512,1024]{2,1,0:T(8,128)(2,1)} %get-tuple-element.23.tile_hbm), custom_call_target="tpu_custom_call" | custom-call | flops 1 | bytes 1048576 | tf_op jit(solution)/shard_map/pallas_call | solution.py:329
  90.7 0.1 all-to-all-done.2.got_ref.row_images_ref
  90.8 0.9 shard_map.72
  91.8 14.8 %all_to_all.42.got_ref = f32[16,8,128]{2,1,0:T(8,128)S(1)} all-to-all(f32[16,8,128]{2,1,0:T(8,128)S(1)} %shard_map.72), channel_id=1, replica_groups=mesh['row'=32,'col'=16] {'col'}, dimensions={0} | all-to-all | bytes 131072 | tf_op jit(solution)/shard_map/all_to_all | solution.py:341
  106.5 0.7 shard_map.73
  107.2 5.1 %all-to-all-start.5 = ((f32[32,8,128]{2,1,0:T(8,128)}), f32[32,8,128]{2,1,0:T(8,128)S(1)}, u32[]{:S(2)}, u32[]{:S(2)}) async-start(f32[32,8,128]{2,1,0:T(8,128)} %shard_map.73), calls=%async_computation.5 | async-start | bytes 262144 | tf_op jit(solution)/shard_map/all_to_all | solution.py:341
  112.3 1.1 shard_map.74
  113.4 8.1 %all-to-all-done.5.got_ref = f32[32,8,128]{2,1,0:T(8,128)S(1)} async-done(((f32[32,8,128]{2,1,0:T(8,128)}), f32[32,8,128]{2,1,0:T(8,128)S(1)}, u32[]{:S(2)}, u32[]{:S(2)}) %all-to-all-start.5) | async-done | bytes 131104 | tf_op jit(solution)/shard_map/all_to_all | solution.py:341
  121.5 10.1 %shard_map.75 = (f32[31,32]{1,0:T(8,128)}, f32[1,128]{1,0:T(1,128)S(1)}) custom-call(f32[32,8,128]{2,1,0:T(8,128)S(1)} %all-to-all-done.5.got_ref, f32[32,128]{1,0:T(8,128)S(1)} %get-tuple-element.24.coef_ref, f32[24,128]{1,0:T(8,128)S(1)} %get-tuple-element.17.own_ref, f32[8,128]{1,0:T(8,128)S(1)} %get-tuple-element.21.own_images_ref, ...), custom_call_target="tpu_custom_call" | custom-call | flops 1 | bytes 1048576 | tf_op jit(solution)/shard_map/pallas_call | solution.py:329
  131.6 11.5 %all_to_all.43 = f32[16,1,128]{2,1,0:T(1,128)S(1)} all-to-all(f32[16,1,128]{2,1,0:T(1,128)S(1)} %broadcast_in_dim.27), channel_id=1, replica_groups=mesh['row'=32,'col'=16] {'col'}, dimensions={0} | all-to-all | bytes 16384 | tf_op jit(solution)/shard_map/all_to_all | solution.py:341
  143.2 11.9 %all_to_all.44 = f32[32,1,128]{2,1,0:T(1,128)S(1)} all-to-all(f32[32,1,128]{2,1,0:T(1,128)S(1)} %broadcast_in_dim.28), channel_id=1, replica_groups=mesh['row'=32,'col'=16] {'row'}, dimensions={0} | all-to-all | bytes 32768 | tf_op jit(solution)/shard_map/all_to_all | solution.py:341
  155.1 0.5 slice_bitcast_fusion
  (5 shorter events, 0.1 us)
Async XLA Ops:
  5.0 35.0 %all-to-all-start = ((f32[32,24,128]{2,1,0:T(8,128)}), f32[32,24,128]{2,1,0:T(8,128)S(1)}, u32[]{:S(2)}, u32[]{:S(2)}) async-start(f32[32,24,128]{2,1,0:T(8,128)} %get-tuple-element.18), calls=%async_computation | async-start | bytes 786432 | tf_op jit(solution)/shard_map/all_to_all | solution.py:341
  78.0 12.8 %all-to-all-start.2 = ((f32[16,8,128]{2,1,0:T(8,128)}), f32[16,8,128]{2,1,0:T(8,128)S(1)}, u32[]{:S(2)}, u32[]{:S(2)}) async-start(f32[16,8,128]{2,1,0:T(8,128)} %get-tuple-element.20), calls=%async_computation.2 | async-start | bytes 131072 | tf_op jit(solution)/shard_map/all_to_all | solution.py:341
  107.2 14.3 %all-to-all-start.5 = ((f32[32,8,128]{2,1,0:T(8,128)}), f32[32,8,128]{2,1,0:T(8,128)S(1)}, u32[]{:S(2)}, u32[]{:S(2)}) async-start(f32[32,8,128]{2,1,0:T(8,128)} %shard_map.73), calls=%async_computation.5 | async-start | bytes 262144 | tf_op jit(solution)/shard_map/all_to_all | solution.py:341

commit v6 on v5

--- a/solution.py
+++ b/solution.py
@@ -16,7 +16,7 @@
 bf16 = jnp.bfloat16
 root_five = 5.0**0.5
 highest = lax.Precision.HIGHEST
-NEAR, LARGE = 16 * 1024 * 1024, 50 * 1024 * 1024
+NEAR, LARGE, WHOLE = 16 * 1024 * 1024, 50 * 1024 * 1024, 60 * 1024 * 1024
 
 
 def dot(left, right, left_dim=1, right_dim=0):
@@ -133,29 +133,43 @@
     return by_high[:, :PAD] + (by_high[:, PAD : 2 * PAD] + by_mid[:, :PAD] + small)
 
 
-def start_kernel(joined_ref, own_ref, col_ref):
-    scaled = joined_ref[0:32, :FEAT] / joined_ref[63:64, :FEAT]
-    down, _ = places()
-    rhs = jnp.where(down < COLS, joined_ref[32:64, :PAD], 0.0).T
+def start_kernel(
+    points_hbm, probes_hbm, targets_hbm, lengths_hbm, variances_hbm,
+    own_ref, col_ref,
+    points_ref, probes_ref, targets_ref, lengths_ref, variances_ref, sems,
+):
+    sources = (points_hbm, probes_hbm, targets_hbm, lengths_hbm, variances_hbm)
+    targets = (points_ref, probes_ref, targets_ref, lengths_ref, variances_ref)
+    copies = [pltpu.make_async_copy(a, b, sems.at[n]) for n, (a, b) in enumerate(zip(sources, targets))]
+    for copy in copies:
+        copy.start()
+    for copy in copies:
+        copy.wait()
+    scaled = points_ref[...] / lengths_ref[...]
+    rhs = jnp.concatenate([probes_ref[...], targets_ref[...], jnp.zeros((1, PAD), f32)], 0).T
     pairs = [jnp.concatenate([scaled[16 * g : 16 * g + 8], scaled[16 * g + 8 : 16 * g + 16]], 1) for g in range(2)]
     block = jnp.concatenate(pairs + [pack(rhs)], 0)
-    own_ref[...] = block
+    scalars = jnp.concatenate([variances_ref[...], jnp.zeros((1, 126), f32)], 1)
+    own_ref[...] = jnp.concatenate([block, jnp.broadcast_to(scalars, (8, 128))], 0)
     col_ref[...] = jnp.broadcast_to(block[None], col_ref.shape)
 
 
-def variances_of(joined_ref):
-    return joined_ref[64:65, 0:1], joined_ref[64:65, 1:2]
+def variances_of(own_ref):
+    return own_ref[8:9, 0:1], own_ref[8:9, 1:2]
 
 
 def norm_lanes(points, first):
-    across = lax.broadcasted_iota(jnp.int32, (points.shape[0], 128), 1)
+    squares = jnp.concatenate(pieces_of(points * points), 1)
+    norms = bdot(squares, jnp.ones((squares.shape[1], 128), bf16))
+    across = lax.broadcasted_iota(jnp.int32, norms.shape, 1)
     lanes = jnp.where((across >= 3 - first) & (across < 6 - first), 1.0, 0.0)
-    for n, piece in enumerate(pieces_of(jnp.sum(points * points, 1, keepdims=True))):
+    for n, piece in enumerate(pieces_of(norms)):
         lanes = jnp.where(across == first + n, piece.astype(f32), lanes)
     return lanes.astype(bf16)
 
 
-def tile_kernel(row_ref, col_ref, own_ref, tile_hbm, message_ref, work_ref, tile_ref, sems):
+def tile_kernel(row_ref, col_ref, tile_hbm, message_ref, own_ref, work_ref, tile_ref, sems):
+    own_ref[...] = row_ref[lax.axis_index("col"), 16:32, :]
     row_points = unpack_points(row_ref) * root_five
     col_points = unpack_points(col_ref) * root_five
     left = jnp.concatenate([left_pieces(row_points), norm_lanes(row_points, 0)], 1)
@@ -183,7 +197,7 @@
         copies[n].start()
     row_rhs = unpack_columns(row_ref, 16)
     col_rhs = unpack_columns(col_ref, 16)
-    own_rhs = unpack(own_ref[16:24, :])
+    own_rhs = unpack(own_ref[0:8, :])
     partial = tile_dot(tile_ref, col_rhs)
     curvature = dot(row_rhs, partial, 0, 0)
     gram = dot(own_rhs, own_rhs, 0, 0)
@@ -196,29 +210,40 @@
         copy.wait()
 
 
-def images_kernel(got_ref, own_ref, joined_ref, own_images_ref, row_ref, col_ref):
-    signal_var, noise_var = variances_of(joined_ref)
+def images_kernel(got_ref, own_ref, own_images_ref, row_ref, col_ref):
+    signal_var, noise_var = variances_of(own_ref)
     summed = jnp.sum(got_ref[...], 0)
-    images = signal_var * summed[0:8] + noise_var * own_ref[16:24, :]
+    images = signal_var * summed[0:8] + noise_var * own_ref[0:8, :]
     own_images_ref[...] = images
     row_ref[...] = jnp.broadcast_to(images[None], row_ref.shape)
     col_ref[...] = jnp.broadcast_to(jnp.concatenate([images, summed[8:16]], 0)[None], col_ref.shape)
 
 
 def residual_of(rhs, images, advance):
-    return rhs - wide_dot(images, advance)
-
-
-def advance_kernel(got_ref, col_ref, joined_ref, tile_hbm, coef_ref, product_ref, tile_ref, sems):
+    wide = jnp.concatenate([advance] * 4, 1)
+    down, across = places(4 * PAD, 4 * PAD)
+    repeated = jnp.where(down // PAD == across // PAD, jnp.concatenate([wide] * 4, 0), 0.0)
+    return rhs - wide_dot(images, repeated)
+
+
+def unpack_values(values):
+    return jnp.concatenate([values[:, PAD * g : PAD * g + PAD] for g in range(4)], 0)
+
+
+def packed_rows(ref, start):
+    return ref[:, start : start + 8, :].reshape(8 * ref.shape[0], 128)
+
+
+def advance_kernel(got_ref, col_ref, own_ref, tile_hbm, coef_ref, product_ref, tile_ref, sems):
     copy = pltpu.make_async_copy(tile_hbm.at[0:3], tile_ref, sems.at[0])
     copy.start()
-    signal_var, noise_var = variances_of(joined_ref)
+    signal_var, noise_var = variances_of(own_ref)
     base_curvature, res_gram = part_symmetric(unpack(jnp.sum(got_ref[:, 8:16, :], 0)))
     curvature = signal_var * base_curvature + noise_var * res_gram
     advance, inverse = eliminate(
         [jnp.concatenate([curvature, res_gram], 1), jnp.concatenate([res_gram, identity()], 1)]
     )
-    residual = residual_of(unpack_columns(col_ref, 16), unpack_columns(got_ref, 0), advance)
+    residual = unpack_values(residual_of(packed_rows(col_ref, 16), packed_rows(got_ref, 0), advance))
     copy.wait()
     product_ref[...] = tile_dot(tile_ref, residual)
     middle = dot(inverse, dot(curvature, inverse))
@@ -227,8 +252,8 @@
 
 def grams_kernel(got_ref, row_ref, own_ref, own_images_ref, coef_ref, product_ref, message_ref):
     advance = coef_ref[:, :PAD]
-    residual = residual_of(unpack_columns(row_ref, 16), unpack_columns(got_ref, 0), advance)
-    own_res = residual_of(unpack(own_ref[16:24, :]), unpack(own_images_ref[...]), advance)
+    residual = unpack_values(residual_of(packed_rows(row_ref, 16), packed_rows(got_ref, 0), advance))
+    own_res = unpack(residual_of(own_ref[0:8, :], own_images_ref[...], advance))
     curvature = dot(residual, product_ref[...], 0, 0)
     gram = dot(own_res, own_res, 0, 0)
     message = pack(join_symmetric(symmetric(curvature), gram))
@@ -255,7 +280,6 @@
     coef_ref,
     own_ref,
     own_images_ref,
-    joined_ref,
     left_ref,
     right_ref,
     points_ref,
@@ -273,10 +297,10 @@
     for n, k in enumerate((0, 1, 3, 4)):
         copies.append(pltpu.make_async_copy(tile_hbm.at[k], tile_ref.at[n], sems.at[n]))
         copies[n].start()
-    signal_var, noise_var = variances_of(joined_ref)
+    signal_var, noise_var = variances_of(own_ref)
     advance, inverse, middle = (coef_ref[:, PAD * g : PAD * g + PAD] for g in range(3))
     base_curvature, next_gram = part_symmetric(unpack(jnp.sum(got_ref[...], 0)))
-    next_curv = signal_var * base_curvature + noise_var * next_gram - symmetric(dot(dot(next_gram, middle), next_gram))
+    next_curv = signal_var * base_curvature + noise_var * next_gram - dot(dot(next_gram, middle), next_gram)
     carry_over = dot(inverse, next_gram)
     (next_advance,) = eliminate([jnp.concatenate([next_curv, next_gram], 1)])
     coef = wide_dot(jnp.concatenate([identity() + carry_over, -advance], 0), next_advance)
@@ -290,7 +314,7 @@
     left = bdot(left_ref[...], right_pieces(form, 0))
     matrix_ref[...] = bdot(left_pieces(left), right_ref[...], 1)
 
-    own_rhs = unpack(own_ref[16:24, :])
+    own_rhs = unpack(own_ref[0:8, :])
     own_solves = dot(jnp.concatenate([own_rhs, unpack(own_images_ref[...])], 1), coef)
     solves_ref[...] = own_solves.T[0:COLS, :]
     pair = jnp.where(across[:PAD] < PROBES, own_rhs, own_solves)
@@ -307,14 +331,17 @@
         upper = weighted.astype(bf16)
         weighted_ref[0, here, :] = upper
         weighted_ref[1, here, :] = (weighted - upper.astype(f32)).astype(bf16)
-        sums_ref[here, :] = jnp.broadcast_to(jnp.sum(weighted, 1, keepdims=True), (16, 128))
+        sums_ref[here, :] = sum(weighted[:, 128 * g : 128 * g + 128] for g in range(weighted.shape[1] // 128))
         return total + values * (high + mid)
 
     signal = lax.fori_loop(0, matrix_ref.shape[0] // 16, strip, jnp.zeros((16, matrix_ref.shape[1]), f32))
     by_upper = bdot(weighted_ref[0], moments_ref[...])
     moved = by_upper[:, :128] + (by_upper[:, 128:] + bdot(weighted_ref[1], moments_ref[:, :128]))
+    sums_high, sums_low = pieces_of(sums_ref[...], 2)
+    ones = jnp.ones((128, 128), bf16)
+    row_sums = bdot(sums_high, ones) + bdot(sums_low, ones)
     points = points_ref[...]
-    scales = points * (points * sums_ref[:, :FEAT] - 2.0 * moved[:, :FEAT]) + moved[:, FEAT:128]
+    scales = points * (points * row_sums[:, :FEAT] - 2.0 * moved[:, :FEAT]) + moved[:, FEAT:128]
     scale_terms = (5.0 / 3.0 * signal_var) * jnp.sum(scales, 0, keepdims=True)
     signal_term = signal_var * jnp.sum(jnp.sum(signal, 0, keepdims=True), 1, keepdims=True)
     terms_ref[...] = jnp.concatenate([scale_terms, signal_term, noise_term, jnp.zeros((1, FEAT - 2), f32)], 1)
@@ -350,20 +377,32 @@
     tile = (row_block, col_set)
     sems = pltpu.SemaphoreType.DMA((4,))
 
-    def widen(array):
-        return jnp.pad(array, ((0, 0), (0, 128 - array.shape[1])))
-
-    parts = (points.T, probe_vectors, targets[None], length_scales[None], variances[None])
-    joined = jnp.concatenate([widen(a) for a in parts], 0)
-    own, to_col = call(start_kernel, [shape_of(24, 128), shape_of(rows, 24, 128)], joined)
+    to_row, to_col = call(
+        start_kernel,
+        [shape_of(32, 128), shape_of(rows, 24, 128)],
+        points.T,
+        probe_vectors,
+        targets[None],
+        length_scales[None],
+        variances[None],
+        far_in=5,
+        limit=WHOLE,
+        scratch=[
+            pltpu.VMEM((width, FEAT), f32),
+            pltpu.VMEM((PROBES, width), f32),
+            pltpu.VMEM((1, width), f32),
+            pltpu.VMEM((1, FEAT), f32),
+            pltpu.VMEM((1, 2), f32),
+            pltpu.SemaphoreType.DMA((5,)),
+        ],
+    )
     col_got = exchange(to_col, "row")
-    row_got = lax.all_gather(own, "col")
-    stack, message = call(
+    row_got = lax.all_gather(to_row, "col")
+    stack, message, own = call(
         tile_kernel,
-        [shape_of(5, *tile, dtype=bf16), shape_of(cols, 16, 128)],
+        [shape_of(5, *tile, dtype=bf16), shape_of(cols, 16, 128), shape_of(16, 128)],
         row_got,
         col_got,
-        own,
         far_outs=1,
         limit=LARGE,
         scratch=[pltpu.VMEM(tile, f32), pltpu.VMEM((5,) + tile, bf16), sems],
@@ -373,7 +412,6 @@
         [shape_of(8, 128), shape_of(cols, 8, 128), shape_of(rows, 16, 128)],
         exchange(message, "col"),
         own,
-        joined,
     )
     col_images = exchange(images_col, "row")
     row_images = exchange(images_row, "col")
@@ -382,7 +420,7 @@
         [shape_of(PAD, 128), shape_of(row_block, PAD)],
         col_images,
         col_got,
-        joined,
+        own,
         stack,
         far_in=1,
         limit=LARGE,
@@ -412,7 +450,6 @@
         coef,
         own,
         own_images,
-        joined,
         *prepared,
         stack,
         far_in=1,

time: 156 us -> 151 us (0.968)
  local copies, waits for them, and re-layouts: 4 us -> 0.53 us
  Pallas kernels: 27.5 us -> 25.1 us
    pad x5 -> x0, local copies, waits for them, and re-layouts: 3.42 us -> none  [widen(): return jnp.pad(array, ((0, 0), (0, 128 - array.shape[1])))]
    pallas_call x8, Pallas kernels: 27.5 us -> 25.1 us  [call(): pl.pallas_call(kernel, out_shape=outs, in_specs=[near] * (len(operands) -...]
  transfers between devices with their start and end apart: 3 -> 3, of which waited for: 2 -> 2; matrix products, arithmetic and copies ran while one was open for 0% -> 0% of each run, Pallas kernels for 6% -> 5%
where the time goes in v6:
time: 151 us; the launch traced here: 150 us
  blocking collectives  94.2 us (62%)
  Pallas kernels  25.1 us (17%)
  starting transfers between devices  20.6 us (14%)
  waiting for transfers between devices  8.96 us (6%)
    all_to_all x5, blocking collectives, exchange(): return lax.all_to_all(blocks, axis, 0, 0, tiled=True)  69.3 us
    pallas_call x8, Pallas kernels, call(): pl.pallas_call(kernel, out_shape=outs, in_specs=[near] * (len(operands) -...  25.1 us
    all_gather x1, blocking collectives, local(): row_got = lax.all_gather(to_row, 'col')  24.9 us
    all_to_all x3, starting transfers between devices, exchange(): return lax.all_to_all(blocks, axis, 0, 0, tiled=True)  20.6 us
    all_to_all x3, waiting for transfers between devices, exchange(): return lax.all_to_all(blocks, axis, 0, 0, tiled=True)  8.96 us
  transfers between devices with their start and end apart: 3, of which 2 were waited for; matrix products, arithmetic and copies ran while one was open for 0% of the time, Pallas kernels for 5%

profile of v6, /device:TPU:1, one launch (start us, length us, event | category | flops | bytes accessed | tf_op | source)
XLA Modules:
  0.0 150.2 jit_solution(13231225599311345903)
XLA Ops:
  0.6 1.7 %shard_map.68 = (f32[32,128]{1,0:T(8,128)}, f32[32,24,128]{2,1,0:T(8,128)}) custom-call(f32[32,64]{1,0:T(8,128)} %bitcast.17, f32[30,32]{1,0:T(8,128)} %probes_hbm.1, f32[1,32]{1,0:T(1,128)} %bitcast.18, f32[1,64]{1,0:T(1,128)} %bitcast.19, f32[1,2]{1,0:T(1,128)} %bitcast.20), custom_call_target="tpu_custom_call" | custom-call | flops 1 | bytes 1048576 | tf_op jit(solution)/shard_map/pallas_call | solution.py:356
  2.3 10.5 %all-to-all-start = ((f32[32,24,128]{2,1,0:T(8,128)}), f32[32,24,128]{2,1,0:T(8,128)S(1)}, u32[]{:S(2)}, u32[]{:S(2)}) async-start(f32[32,24,128]{2,1,0:T(8,128)} %get-tuple-element.19), calls=%async_computation | async-start | bytes 786432 | tf_op jit(solution)/shard_map/all_to_all | solution.py:368
  12.9 24.9 %all-gather = f32[512,128]{1,0:T(8,128)S(1)} all-gather(f32[32,128]{1,0:T(8,128)} %get-tuple-element.18), channel_id=2, replica_groups=mesh['row'=32,'col'=16] {'col'}, dimensions={0}, use_global_device_ids=true | all-gather | bytes 278528 | tf_op jit(solution)/shard_map/all_gather | solution.py:400
  37.8 0.0 all-to-all-done.col_ref
  37.8 5.1 %shard_map.69 = (bf16[5,512,1024]{2,1,0:T(8,128)(2,1)}, f32[16,16,128]{2,1,0:T(8,128)S(1)}, f32[16,128]{1,0:T(8,128)S(1)}) custom-call(f32[16,32,128]{2,1,0:T(8,128)S(1)} %bitcast.11, f32[32,24,128]{2,1,0:T(8,128)S(1)} %all-to-all-done.col_ref), custom_call_target="tpu_custom_call" | custom-call | flops 1 | bytes 1048576 | tf_op jit(solution)/shard_map/pallas_call | solution.py:356
  42.8 11.9 %all_to_all.40.got_ref = f32[16,16,128]{2,1,0:T(8,128)S(1)} all-to-all(f32[16,16,128]{2,1,0:T(8,128)S(1)} %get-tuple-element.20), channel_id=1, replica_groups=mesh['row'=32,'col'=16] {'col'}, dimensions={0} | all-to-all | bytes 262144 | tf_op jit(solution)/shard_map/all_to_all | solution.py:368
  54.7 0.7 shard_map.70
  55.4 20.0 %all_to_all.41.got_ref.col_images_ref = f32[32,16,128]{2,1,0:T(8,128)S(1)} all-to-all(f32[32,16,128]{2,1,0:T(8,128)S(1)} %get-tuple-element.24), channel_id=1, replica_groups=mesh['row'=32,'col'=16] {'row'}, dimensions={0} | all-to-all | bytes 524288 | tf_op jit(solution)/shard_map/all_to_all | solution.py:368
  75.4 5.0 %all-to-all-start.2 = ((f32[16,8,128]{2,1,0:T(8,128)}), f32[16,8,128]{2,1,0:T(8,128)S(1)}, u32[]{:S(2)}, u32[]{:S(2)}) async-start(f32[16,8,128]{2,1,0:T(8,128)} %get-tuple-element.22), calls=%async_computation.2 | async-start | bytes 131072 | tf_op jit(solution)/shard_map/all_to_all | solution.py:368
  80.4 6.9 %shard_map.71 = (f32[32,128]{1,0:T(8,128)S(1)}, f32[512,32]{1,0:T(8,128)S(1)}) custom-call(f32[32,16,128]{2,1,0:T(8,128)S(1)} %all_to_all.41.got_ref.col_images_ref, f32[32,24,128]{2,1,0:T(8,128)S(1)} %all-to-all-done.col_ref, f32[16,128]{1,0:T(8,128)S(1)} %get-tuple-element.21.own_ref, bf16[5,512,1024]{2,1,0:T(8,128)(2,1)} %get-tuple-element.25.tile_hbm), custom_call_target="tpu_custom_call" | custom-call | flops 1 | bytes 1048576 | tf_op jit(solution)/shard_map/pallas_call | solution.py:356
  87.4 0.9 all-to-all-done.2.got_ref.row_images_ref
  88.3 0.8 shard_map.72
  89.1 14.0 %all_to_all.42.got_ref = f32[16,8,128]{2,1,0:T(8,128)S(1)} all-to-all(f32[16,8,128]{2,1,0:T(8,128)S(1)} %shard_map.72), channel_id=1, replica_groups=mesh['row'=32,'col'=16] {'col'}, dimensions={0} | all-to-all | bytes 131072 | tf_op jit(solution)/shard_map/all_to_all | solution.py:368
  103.1 0.7 shard_map.73
  103.8 5.1 %all-to-all-start.5 = ((f32[32,8,128]{2,1,0:T(8,128)}), f32[32,8,128]{2,1,0:T(8,128)S(1)}, u32[]{:S(2)}, u32[]{:S(2)}) async-start(f32[32,8,128]{2,1,0:T(8,128)} %shard_map.73), calls=%async_computation.5 | async-start | bytes 262144 | tf_op jit(solution)/shard_map/all_to_all | solution.py:368
  108.9 1.1 shard_map.74
  110.0 8.1 %all-to-all-done.5.got_ref = f32[32,8,128]{2,1,0:T(8,128)S(1)} async-done(((f32[32,8,128]{2,1,0:T(8,128)}), f32[32,8,128]{2,1,0:T(8,128)S(1)}, u32[]{:S(2)}, u32[]{:S(2)}) %all-to-all-start.5) | async-done | bytes 131104 | tf_op jit(solution)/shard_map/all_to_all | solution.py:368
  118.0 8.1 %shard_map.75 = (f32[31,32]{1,0:T(8,128)}, f32[1,128]{1,0:T(1,128)S(1)}) custom-call(f32[32,8,128]{2,1,0:T(8,128)S(1)} %all-to-all-done.5.got_ref, f32[32,128]{1,0:T(8,128)S(1)} %get-tuple-element.26.coef_ref, f32[16,128]{1,0:T(8,128)S(1)} %get-tuple-element.21.own_ref, f32[8,128]{1,0:T(8,128)S(1)} %get-tuple-element.23.own_images_ref, ...), custom_call_target="tpu_custom_call" | custom-call | flops 1 | bytes 1048576 | tf_op jit(solution)/shard_map/pallas_call | solution.py:356
  126.2 11.5 %all_to_all.43 = f32[16,1,128]{2,1,0:T(1,128)S(1)} all-to-all(f32[16,1,128]{2,1,0:T(1,128)S(1)} %broadcast_in_dim.27), channel_id=1, replica_groups=mesh['row'=32,'col'=16] {'col'}, dimensions={0} | all-to-all | bytes 16384 | tf_op jit(solution)/shard_map/all_to_all | solution.py:368
  137.7 11.9 %all_to_all.44 = f32[32,1,128]{2,1,0:T(1,128)S(1)} all-to-all(f32[32,1,128]{2,1,0:T(1,128)S(1)} %broadcast_in_dim.28), channel_id=1, replica_groups=mesh['row'=32,'col'=16] {'row'}, dimensions={0} | all-to-all | bytes 32768 | tf_op jit(solution)/shard_map/all_to_all | solution.py:368
  149.7 0.5 slice_bitcast_fusion
  (4 shorter events, 0.1 us)
Async XLA Ops:
  2.3 35.4 %all-to-all-start = ((f32[32,24,128]{2,1,0:T(8,128)}), f32[32,24,128]{2,1,0:T(8,128)S(1)}, u32[]{:S(2)}, u32[]{:S(2)}) async-start(f32[32,24,128]{2,1,0:T(8,128)} %get-tuple-element.19), calls=%async_computation | async-start | bytes 786432 | tf_op jit(solution)/shard_map/all_to_all | solution.py:368
  75.4 12.8 %all-to-all-start.2 = ((f32[16,8,128]{2,1,0:T(8,128)}), f32[16,8,128]{2,1,0:T(8,128)S(1)}, u32[]{:S(2)}, u32[]{:S(2)}) async-start(f32[16,8,128]{2,1,0:T(8,128)} %get-tuple-element.22), calls=%async_computation.2 | async-start | bytes 131072 | tf_op jit(solution)/shard_map/all_to_all | solution.py:368
  103.8 14.3 %all-to-all-start.5 = ((f32[32,8,128]{2,1,0:T(8,128)}), f32[32,8,128]{2,1,0:T(8,128)S(1)}, u32[]{:S(2)}, u32[]{:S(2)}) async-start(f32[32,8,128]{2,1,0:T(8,128)} %shard_map.73), calls=%async_computation.5 | async-start | bytes 262144 | tf_op jit(solution)/shard_map/all_to_all | solution.py:368

commit v7 on v6

--- a/solution.py
+++ b/solution.py
@@ -210,12 +210,11 @@
         copy.wait()
 
 
-def images_kernel(got_ref, own_ref, own_images_ref, row_ref, col_ref):
+def images_kernel(got_ref, own_ref, own_images_ref, col_ref):
     signal_var, noise_var = variances_of(own_ref)
     summed = jnp.sum(got_ref[...], 0)
     images = signal_var * summed[0:8] + noise_var * own_ref[0:8, :]
     own_images_ref[...] = images
-    row_ref[...] = jnp.broadcast_to(images[None], row_ref.shape)
     col_ref[...] = jnp.broadcast_to(jnp.concatenate([images, summed[8:16]], 0)[None], col_ref.shape)
 
 
@@ -234,33 +233,34 @@
     return ref[:, start : start + 8, :].reshape(8 * ref.shape[0], 128)
 
 
-def advance_kernel(got_ref, col_ref, own_ref, tile_hbm, coef_ref, product_ref, tile_ref, sems):
+def grams_kernel(
+    col_images_ref, row_images_ref, col_ref, row_ref, own_ref, own_images_ref, tile_hbm, coef_ref, message_ref, tile_ref, sems
+):
     copy = pltpu.make_async_copy(tile_hbm.at[0:3], tile_ref, sems.at[0])
     copy.start()
     signal_var, noise_var = variances_of(own_ref)
-    base_curvature, res_gram = part_symmetric(unpack(jnp.sum(got_ref[:, 8:16, :], 0)))
+    base_curvature, res_gram = part_symmetric(unpack(jnp.sum(col_images_ref[:, 8:16, :], 0)))
     curvature = signal_var * base_curvature + noise_var * res_gram
-    advance, inverse = eliminate(
-        [jnp.concatenate([curvature, res_gram], 1), jnp.concatenate([res_gram, identity()], 1)]
-    )
-    residual = unpack_values(residual_of(packed_rows(col_ref, 16), packed_rows(got_ref, 0), advance))
+    (advance,) = eliminate([jnp.concatenate([curvature, res_gram], 1)])
+    coef_ref[...] = jnp.concatenate([advance, res_gram, curvature, jnp.zeros((PAD, PAD), f32)], 1)
+    col_res = unpack_values(residual_of(packed_rows(col_ref, 16), packed_rows(col_images_ref, 0), advance))
+    row_res = unpack_values(residual_of(packed_rows(row_ref, 16), packed_rows(row_images_ref, 0), advance))
+    own_res = unpack(residual_of(own_ref[0:8, :], own_images_ref[...], advance))
     copy.wait()
-    product_ref[...] = tile_dot(tile_ref, residual)
+    product = tile_dot(tile_ref, col_res)
+    next_curvature = dot(row_res, product, 0, 0)
+    next_gram = dot(own_res, own_res, 0, 0)
+    message = pack(join_symmetric(symmetric(next_curvature), next_gram))
+    message_ref[...] = jnp.broadcast_to(message[None], message_ref.shape)
+
+
+def prepare_kernel(
+    coef_ref, row_ref, col_ref, row_images_ref, col_images_ref, left_ref, right_ref, points_ref, moments_ref, out_ref
+):
+    advance, res_gram, curvature = (coef_ref[:, PAD * g : PAD * g + PAD] for g in range(3))
+    (inverse,) = eliminate([jnp.concatenate([res_gram, identity()], 1)])
     middle = dot(inverse, dot(curvature, inverse))
-    coef_ref[...] = jnp.concatenate([advance, inverse, symmetric(middle), jnp.zeros((PAD, PAD), f32)], 1)
-
-
-def grams_kernel(got_ref, row_ref, own_ref, own_images_ref, coef_ref, product_ref, message_ref):
-    advance = coef_ref[:, :PAD]
-    residual = unpack_values(residual_of(packed_rows(row_ref, 16), packed_rows(got_ref, 0), advance))
-    own_res = unpack(residual_of(own_ref[0:8, :], own_images_ref[...], advance))
-    curvature = dot(residual, product_ref[...], 0, 0)
-    gram = dot(own_res, own_res, 0, 0)
-    message = pack(join_symmetric(symmetric(curvature), gram))
-    message_ref[...] = jnp.broadcast_to(message[None], message_ref.shape)
-
-
-def prepare_kernel(row_ref, col_ref, row_images_ref, col_images_ref, left_ref, right_ref, points_ref, moments_ref):
+    out_ref[...] = jnp.concatenate([advance, inverse, symmetric(middle), jnp.zeros((PAD, PAD), f32)], 1)
     left_ref[...] = left_pieces(jnp.concatenate([unpack_columns(row_ref, 16), unpack_columns(row_images_ref, 0)], 1))
     right = jnp.concatenate([unpack_columns(col_ref, 16), unpack_columns(col_images_ref, 0)], 1)
     right_ref[...] = right_pieces(right, 1)
@@ -407,36 +407,35 @@
         limit=LARGE,
         scratch=[pltpu.VMEM(tile, f32), pltpu.VMEM((5,) + tile, bf16), sems],
     )
-    own_images, images_row, images_col = call(
-        images_kernel,
-        [shape_of(8, 128), shape_of(cols, 8, 128), shape_of(rows, 16, 128)],
-        exchange(message, "col"),
+    own_images, images_col = call(
+        images_kernel, [shape_of(8, 128), shape_of(rows, 16, 128)], exchange(message, "col"), own
+    )
+    col_images = exchange(images_col, "row")
+    row_images = lax.all_gather(own_images, "col")
+    coef, message = call(
+        grams_kernel,
+        [shape_of(PAD, 128), shape_of(cols, 8, 128)],
+        col_images,
+        row_images,
+        col_got,
+        row_got,
         own,
-    )
-    col_images = exchange(images_col, "row")
-    row_images = exchange(images_row, "col")
-    coef, product = call(
-        advance_kernel,
-        [shape_of(PAD, 128), shape_of(row_block, PAD)],
-        col_images,
-        col_got,
-        own,
+        own_images,
         stack,
         far_in=1,
         limit=LARGE,
         scratch=[pltpu.VMEM((3,) + tile, bf16), sems],
     )
-    (message,) = call(
-        grams_kernel, [shape_of(cols, 8, 128)], row_images, row_got, own, own_images, coef, product
-    )
-    prepared = call(
+    *prepared, coef = call(
         prepare_kernel,
         [
             shape_of(row_block, 12 * PAD, dtype=bf16),
             shape_of(col_set, 12 * PAD, dtype=bf16),
             shape_of(row_block, FEAT),
             shape_of(col_set, 4 * FEAT, dtype=bf16),
+            shape_of(PAD, 128),
         ],
+        coef,
         row_got,
         col_got,
         row_images,
@@ -463,8 +462,8 @@
         ],
     )
     terms = jnp.sum(exchange(jnp.broadcast_to(terms[None], (cols, 1, 128)), "col"), 0)
-    terms = jnp.sum(exchange(jnp.broadcast_to(terms[None], (rows, 1, 128)), "row"), 0)
-    return (solves, terms[0, : FEAT + 2])
+    terms = exchange(jnp.broadcast_to(terms[None], (rows, 1, 128)), "row")
+    return (solves, jnp.sum(terms[:, 0, : FEAT + 2], 0))
 
 
 def solution(mesh):

time: 151 us -> 151 us (level)
  starting transfers between devices: 20.6 us -> 29.5 us
  blocking collectives: 94.2 us -> 87.4 us
  waiting for transfers between devices: 8.96 us -> 5.66 us
  Pallas kernels: 25.1 us -> 26.9 us
    all_to_all x5 -> x4, blocking collectives: 69.3 us -> 47.8 us  [exchange(): return lax.all_to_all(blocks, axis, 0, 0, tiled=True)]
    all_gather x0 -> x1, blocking collectives: none -> 14.6 us  [local(): row_images = lax.all_gather(own_images, 'col')]
    all_to_all x3, starting transfers between devices: 20.6 us -> 29.5 us  [exchange(): return lax.all_to_all(blocks, axis, 0, 0, tiled=True)]
    all_to_all x3, waiting for transfers between devices: 8.96 us -> 5.66 us  [exchange(): return lax.all_to_all(blocks, axis, 0, 0, tiled=True)]
    pallas_call x8 -> x7, Pallas kernels: 25.1 us -> 26.9 us  [call(): pl.pallas_call(kernel, out_shape=outs, in_specs=[near] * (len(operands) -...]
  transfers between devices with their start and end apart: 3 -> 3, of which waited for: 2 -> 1; matrix products, arithmetic and copies ran while one was open for 0% -> 0% of each run, Pallas kernels for 5% -> 2%
where the time goes in v7:
time: 151 us
  blocking collectives  87.4 us (58%)
  starting transfers between devices  29.5 us (20%)
  Pallas kernels  26.9 us (18%)
  waiting for transfers between devices  5.66 us (4%)
    all_to_all x4, blocking collectives, exchange(): return lax.all_to_all(blocks, axis, 0, 0, tiled=True)  47.8 us
    all_to_all x3, starting transfers between devices, exchange(): return lax.all_to_all(blocks, axis, 0, 0, tiled=True)  29.5 us
    pallas_call x7, Pallas kernels, call(): pl.pallas_call(kernel, out_shape=outs, in_specs=[near] * (len(operands) -...  26.9 us
    all_gather x1, blocking collectives, local(): row_got = lax.all_gather(to_row, 'col')  24.9 us
    all_gather x1, blocking collectives, local(): row_images = lax.all_gather(own_images, 'col')  14.6 us
    all_to_all x3, waiting for transfers between devices, exchange(): return lax.all_to_all(blocks, axis, 0, 0, tiled=True)  5.66 us
  transfers between devices with their start and end apart: 3, of which 1 were waited for; matrix products, arithmetic and copies ran while one was open for 0% of the time, Pallas kernels for 2%

profile of v7, /device:TPU:1, one launch (start us, length us, event | category | flops | bytes accessed | tf_op | source)
XLA Modules:
  0.0 150.7 jit_solution(14354694531532106600)
XLA Ops:
  0.6 1.7 %shard_map.68 = (f32[32,128]{1,0:T(8,128)}, f32[32,24,128]{2,1,0:T(8,128)}) custom-call(f32[32,64]{1,0:T(8,128)} %bitcast.18, f32[30,32]{1,0:T(8,128)} %probes_hbm.1, f32[1,32]{1,0:T(1,128)} %bitcast.19, f32[1,64]{1,0:T(1,128)} %bitcast.20, f32[1,2]{1,0:T(1,128)} %bitcast.21), custom_call_target="tpu_custom_call" | custom-call | flops 1 | bytes 1048576 | tf_op jit(solution)/shard_map/pallas_call | solution.py:356
  2.3 10.5 %all-to-all-start = ((f32[32,24,128]{2,1,0:T(8,128)}), f32[32,24,128]{2,1,0:T(8,128)S(1)}, u32[]{:S(2)}, u32[]{:S(2)}) async-start(f32[32,24,128]{2,1,0:T(8,128)} %get-tuple-element.19), calls=%async_computation | async-start | bytes 786432 | tf_op jit(solution)/shard_map/all_to_all | solution.py:368
  12.9 24.9 %all-gather = f32[512,128]{1,0:T(8,128)S(1)} all-gather(f32[32,128]{1,0:T(8,128)} %get-tuple-element.18), channel_id=2, replica_groups=mesh['row'=32,'col'=16] {'col'}, dimensions={0}, use_global_device_ids=true | all-gather | bytes 278528 | tf_op jit(solution)/shard_map/all_gather | solution.py:400
  37.8 0.0 all-to-all-done.col_ref
  37.8 5.1 %shard_map.69 = (bf16[5,512,1024]{2,1,0:T(8,128)(2,1)}, f32[16,16,128]{2,1,0:T(8,128)S(1)}, f32[16,128]{1,0:T(8,128)S(1)}) custom-call(f32[16,32,128]{2,1,0:T(8,128)S(1)} %bitcast.10, f32[32,24,128]{2,1,0:T(8,128)S(1)} %all-to-all-done.col_ref), custom_call_target="tpu_custom_call" | custom-call | flops 1 | bytes 1048576 | tf_op jit(solution)/shard_map/pallas_call | solution.py:356
  42.8 11.9 %all_to_all.35.got_ref = f32[16,16,128]{2,1,0:T(8,128)S(1)} all-to-all(f32[16,16,128]{2,1,0:T(8,128)S(1)} %get-tuple-element.20), channel_id=1, replica_groups=mesh['row'=32,'col'=16] {'col'}, dimensions={0} | all-to-all | bytes 262144 | tf_op jit(solution)/shard_map/all_to_all | solution.py:368
  54.7 0.8 shard_map.70
  55.5 9.5 %all-to-all-start.2 = ((f32[32,16,128]{2,1,0:T(8,128)}), f32[32,16,128]{2,1,0:T(8,128)S(1)}, u32[]{:S(2)}, u32[]{:S(2)}) async-start(f32[32,16,128]{2,1,0:T(8,128)} %get-tuple-element.22), calls=%async_computation.2 | async-start | bytes 524288 | tf_op jit(solution)/shard_map/all_to_all | solution.py:368
  65.0 14.6 %all-gather.1 = f32[128,128]{1,0:T(8,128)S(1)} all-gather(f32[8,128]{1,0:T(8,128)S(1)} %get-tuple-element.23.own_images_ref), channel_id=3, replica_groups=mesh['row'=32,'col'=16] {'col'}, dimensions={0}, use_global_device_ids=true | all-gather | bytes 69632 | tf_op jit(solution)/shard_map/all_gather | solution.py:414
  79.7 0.0 all-to-all-done.2.col_images_ref
  79.7 7.0 %shard_map.71 = (f32[32,128]{1,0:T(8,128)S(1)}, f32[16,8,128]{2,1,0:T(8,128)S(1)}) custom-call(f32[32,16,128]{2,1,0:T(8,128)S(1)} %all-to-all-done.2.col_images_ref, f32[16,8,128]{2,1,0:T(8,128)S(1)} %bitcast.13, f32[32,24,128]{2,1,0:T(8,128)S(1)} %all-to-all-done.col_ref, f32[16,32,128]{2,1,0:T(8,128)S(1)} %bitcast.11, ...), custom_call_target="tpu_custom_call" | custom-call | flops 1 | bytes 1048576 | tf_op jit(solution)/shard_map/pallas_call | solution.py:356
  86.7 12.5 %all_to_all.36.got_ref = f32[16,8,128]{2,1,0:T(8,128)S(1)} all-to-all(f32[16,8,128]{2,1,0:T(8,128)S(1)} %get-tuple-element.25), channel_id=1, replica_groups=mesh['row'=32,'col'=16] {'col'}, dimensions={0} | all-to-all | bytes 131072 | tf_op jit(solution)/shard_map/all_to_all | solution.py:368
  99.2 0.7 shard_map.72
  99.9 9.5 %all-to-all-start.4 = ((f32[32,8,128]{2,1,0:T(8,128)}), f32[32,8,128]{2,1,0:T(8,128)S(1)}, u32[]{:S(2)}, u32[]{:S(2)}) async-start(f32[32,8,128]{2,1,0:T(8,128)} %shard_map.72), calls=%async_computation.4 | async-start | bytes 262144 | tf_op jit(solution)/shard_map/all_to_all | solution.py:368
  109.4 3.5 %shard_map.73 = (bf16[512,384]{1,0:T(8,128)(2,1)S(1)}, bf16[1024,384]{1,0:T(8,128)(2,1)S(1)}, f32[512,64]{1,0:T(8,128)S(1)}, bf16[1024,256]{1,0:T(8,128)(2,1)S(1)}, f32[32,128]{1,0:T(8,128)S(1)}) custom-call(f32[32,128]{1,0:T(8,128)S(1)} %get-tuple-element.26.coef_ref, f32[16,32,128]{2,1,0:T(8,128)S(1)} %bitcast.12, ...), custom_call_target="tpu_custom_call" | custom-call | flops 1 | bytes 1048576 | tf_op jit(solution)/shard_map/pallas_call | solution.py:356
  112.9 5.7 %all-to-all-done.4.got_ref = f32[32,8,128]{2,1,0:T(8,128)S(1)} async-done(((f32[32,8,128]{2,1,0:T(8,128)}), f32[32,8,128]{2,1,0:T(8,128)S(1)}, u32[]{:S(2)}, u32[]{:S(2)}) %all-to-all-start.4) | async-done | bytes 131104 | tf_op jit(solution)/shard_map/all_to_all | solution.py:368
  118.6 8.1 %shard_map.74 = (f32[31,32]{1,0:T(8,128)}, f32[1,128]{1,0:T(1,128)S(1)}) custom-call(f32[32,8,128]{2,1,0:T(8,128)S(1)} %all-to-all-done.4.got_ref, f32[32,128]{1,0:T(8,128)S(1)} %get-tuple-element.27.coef_ref, f32[16,128]{1,0:T(8,128)S(1)} %get-tuple-element.21.own_ref, f32[8,128]{1,0:T(8,128)S(1)} %get-tuple-element.23.own_images_ref, ...), custom_call_target="tpu_custom_call" | custom-call | flops 1 | bytes 1048576 | tf_op jit(solution)/shard_map/pallas_call | solution.py:356
  126.7 11.5 %all_to_all.37 = f32[16,1,128]{2,1,0:T(1,128)S(1)} all-to-all(f32[16,1,128]{2,1,0:T(1,128)S(1)} %broadcast_in_dim.27), channel_id=1, replica_groups=mesh['row'=32,'col'=16] {'col'}, dimensions={0} | all-to-all | bytes 16384 | tf_op jit(solution)/shard_map/all_to_all | solution.py:368
  138.3 11.9 %all_to_all.38 = f32[32,1,128]{2,1,0:T(1,128)S(1)} all-to-all(f32[32,1,128]{2,1,0:T(1,128)S(1)} %broadcast_in_dim.28), channel_id=1, replica_groups=mesh['row'=32,'col'=16] {'row'}, dimensions={0} | all-to-all | bytes 32768 | tf_op jit(solution)/shard_map/all_to_all | solution.py:368
  150.2 0.5 reduce_sum.19
  (3 shorter events, 0.0 us)
Async XLA Ops:
  2.3 35.4 %all-to-all-start = ((f32[32,24,128]{2,1,0:T(8,128)}), f32[32,24,128]{2,1,0:T(8,128)S(1)}, u32[]{:S(2)}, u32[]{:S(2)}) async-start(f32[32,24,128]{2,1,0:T(8,128)} %get-tuple-element.19), calls=%async_computation | async-start | bytes 786432 | tf_op jit(solution)/shard_map/all_to_all | solution.py:368
  55.5 24.2 %all-to-all-start.2 = ((f32[32,16,128]{2,1,0:T(8,128)}), f32[32,16,128]{2,1,0:T(8,128)S(1)}, u32[]{:S(2)}, u32[]{:S(2)}) async-start(f32[32,16,128]{2,1,0:T(8,128)} %get-tuple-element.22), calls=%async_computation.2 | async-start | bytes 524288 | tf_op jit(solution)/shard_map/all_to_all | solution.py:368
  99.9 18.7 %all-to-all-start.4 = ((f32[32,8,128]{2,1,0:T(8,128)}), f32[32,8,128]{2,1,0:T(8,128)S(1)}, u32[]{:S(2)}, u32[]{:S(2)}) async-start(f32[32,8,128]{2,1,0:T(8,128)} %shard_map.72), calls=%async_computation.4 | async-start | bytes 262144 | tf_op jit(solution)/shard_map/all_to_all | solution.py:368
